TPU v7x, 32 devices: a whole 2x2x4 slice. The times are simulated.
32 devices in a mesh: dp: 8 (over y, x, core), tensor: 4 (over z).
Axes of the slice: x: 2, y: 2, z: 4, core: 2. Of those that a mesh axis runs over, the one named last changes fastest.
Arguments:
- tokens: bfloat16 [6, 4096, 4096], P(None, 'dp', 'tensor'), may hold values from -16 to 16
- router: bfloat16 [16, 4096], P(None, 'tensor'), may hold values from -32 to 32
- w_gate: bfloat16 [4, 14336, 4096], P('tensor', 'dp'), may hold values from -0.625 to 0.625
- w_up: bfloat16 [4, 14336, 4096], P('tensor', 'dp'), may hold values from -0.625 to 0.625
- w_down: bfloat16 [4, 14336, 4096], P('tensor', 'dp'), may hold values from -0.046875 to 0.046875
Outputs:
- mixed: bfloat16 [6, 4096, 4096], P(None, 'dp', 'tensor')
- log_total: float32 [6, 4096], P(None, 'dp')
All inputs are finite; a program needn't handle non-finite values.
Results may differ from a plain program's by a relative error of at most 0.0096.
Values may be sent and summed in bfloat16 or wider, within the bound.
A program may use at most 128 MiB of HBM per device.

v0:
```python
import jax
import jax.numpy as jnp
from jax import lax
from jax.sharding import PartitionSpec as P

SLOTS = 4


epsilon = 1e-05


def per_device(tokens, router, w_gate, w_up, w_down):
    width_part = tokens.shape[2]
    tensor_count = lax.axis_size("tensor")
    full_width = width_part * tensor_count
    squares = jnp.sum(jnp.square(tokens.astype(jnp.float32)), axis=2)
    raw_logits = jnp.einsum("sd,gtd->gst", router, tokens, preferred_element_type=jnp.float32)
    raw_logits, squares = lax.psum((raw_logits, squares), "tensor")
    norm_scale = lax.rsqrt(squares / full_width + epsilon)
    logits = raw_logits * norm_scale[:, None, :]
    peaks = lax.pmax(jnp.max(logits, axis=2), "dp")
    powers = jnp.exp(logits - peaks[:, :, None])
    local_sum = jnp.sum(powers, axis=2)
    weights = (powers * norm_scale[:, None, :]).astype(jnp.bfloat16)
    partial_value = jnp.einsum("gst,gtd->gsd", weights, tokens, preferred_element_type=jnp.float32)
    column_sum = lax.psum(local_sum, "dp")
    slot_in = lax.psum(partial_value / column_sum[:, :, None], "dp").astype(jnp.bfloat16)
    row_peak = jnp.max(logits, axis=1, keepdims=True)
    row_powers = jnp.exp(logits - row_peak)
    row_sum = jnp.sum(row_powers, axis=1, keepdims=True)
    combine = (row_powers / row_sum).astype(jnp.bfloat16)
    log_total = (row_peak + jnp.log(row_sum))[:, 0, :]
    experts_here = w_gate.shape[0]
    inputs = lax.all_to_all(slot_in, "tensor", split_axis=1, concat_axis=2, tiled=True)
    count = inputs.shape[0]
    grouped = inputs.reshape(count, experts_here, SLOTS, full_width)
    gate_act = jnp.einsum("nksd,kfd->nksf", grouped, w_gate, preferred_element_type=jnp.float32)
    up_act = jnp.einsum("nksd,kfd->nksf", grouped, w_up, preferred_element_type=jnp.float32)
    hidden = (jax.nn.silu(gate_act) * up_act).astype(jnp.bfloat16)
    result = jnp.einsum("nksf,kfd->nksd", hidden, w_down, preferred_element_type=jnp.float32)
    partial_out = result.reshape(count, experts_here * SLOTS, full_width)
    slot_out = lax.psum(partial_out, "dp").astype(jnp.bfloat16)
    window_out = lax.all_to_all(slot_out, "tensor", split_axis=2, concat_axis=1, tiled=True)
    mixed = jnp.einsum(
        "gst,gsd->gtd", combine, window_out, preferred_element_type=jnp.float32
    ).astype(jnp.bfloat16)
    return (mixed, log_total)


def solution(mesh):
    in_specs = (
        P(None, "dp", "tensor"),
        P(None, "tensor"),
        P("tensor", "dp", None),
        P("tensor", "dp", None),
        P("tensor", "dp", None),
    )
    out_specs = (P(None, "dp", "tensor"), P(None, "dp"))
    return jax.shard_map(
        per_device, mesh=mesh, in_specs=in_specs, out_specs=out_specs, check_vma=False
    )
```

profile of v0, /device:TPU:0, one launch (start us, length us, event | category | flops | bytes accessed | tf_op | source)
XLA Modules:
  0.0 224.5 jit_solution(15826406239515512000)
XLA Ops:
  7.2 0.0 copy-start
  7.2 0.0 all-reduce.4.cloned.1.call-start
  7.2 0.7 copy-done
  7.9 5.2 %convolution_bitcast_fusion = f32[6,16,512]{2,1,0:T(8,128)} fusion(bf16[6,512,1024]{2,1,0:T(8,128)(2,1)} %param.5, bf16[16,1024]{1,0:T(8,128)(2,1)S(1)} %copy-done), kind=kOutput, calls=%fused_computation.14 | convolution fusion | flops 100663296 | bytes 6520832 | tf_op jit(solution)/shard_map/sd,gtd->gst/dot_general | solution.py:17
  13.1 0.0 all-reduce.4.cloned.1.call-update
  13.2 4.1 %multiply_reduce_fusion = f32[6,512]{1,0:T(8,128)S(1)} fusion(bf16[6,512,1024]{2,1,0:T(8,128)(2,1)} %param.5), kind=kLoop, calls=%fused_computation.6 | loop fusion | flops 9434112 | bytes 6303744 | tf_op jit(solution)/shard_map/reduce_sum | solution.py:16
  17.2 20.6 %psum.36 = f32[6,512]{1,0:T(8,128)S(1)} all-reduce(f32[6,512]{1,0:T(8,128)S(1)} %multiply_reduce_fusion), channel_id=1, replica_groups=mesh['dp'=8,'tensor'=4] {'tensor'}, use_global_device_ids=true, to_apply=%region_2.0 | all-reduce | flops 3072 | bytes 24576 | tf_op jit(solution)/shard_map/psum | solution.py:18
  37.8 13.1 %all-reduce.4.cloned.1.call-done = f32[6,16,512]{2,1,0:T(8,128)} async-done(((f32[6,16,512]{2,1,0:T(8,128)}), f32[6,16,512]{2,1,0:T(8,128)}) %all-reduce.4.cloned.1.call-update) | async-done | bytes 196624 | tf_op jit(solution)/shard_map/psum | solution.py:18
  51.0 1.0 multiply_reduce_fusion.2
  51.9 1.0 fusion.23
  53.0 11.8 %pmax.7 = f32[6,16]{1,0:T(8,128)S(1)} all-reduce(f32[6,16]{1,0:T(8,128)S(1)} %get-tuple-element.3), channel_id=1, replica_groups=mesh['dp'=8,'tensor'=4] {'dp'}, use_global_device_ids=true, to_apply=%region_6.0 | all-reduce | flops 96 | bytes 768 | tf_op jit(solution)/shard_map/pmax | solution.py:21
  64.8 1.1 fusion.24
  65.9 11.8 %psum.37 = f32[6,16]{1,0:T(8,128)S(1)} all-reduce(f32[6,16]{1,0:T(8,128)S(1)} %fusion.24), channel_id=1, replica_groups=mesh['dp'=8,'tensor'=4] {'dp'}, use_global_device_ids=true, to_apply=%region_8.0 | all-reduce | flops 96 | bytes 768 | tf_op jit(solution)/shard_map/psum | solution.py:26
  77.8 3.9 %convolution_divide_fusion = f32[6,16,1024]{2,1,0:T(8,128)S(1)} fusion(bf16[6,512,1024]{2,1,0:T(8,128)(2,1)} %param.5, f32[6,16]{1,0:T(8,128)S(1)} %psum.37, f32[6,16,512]{2,1,0:T(8,128)} %all-reduce.4.cloned.1.call-done, f32[6,16]{1,0:T(8,128)S(1)} %pmax.7, f32[6,512]{1,0:T(8,128)S(1)} %add_rsqrt_fusion), kind=kOutput, calls=%fused_computation.13 | convolution fusion | flops 100958208 | bytes 6894336 | tf_op jit(solution)/shard_map/gst,gtd->gsd/dot_general | solution.py:25
  81.6 26.8 %all-reduce.5 = bf16[6,16,1024]{2,1,0:T(8,128)(2,1)S(1)} all-reduce(f32[6,16,1024]{2,1,0:T(8,128)S(1)} %convolution_divide_fusion), channel_id=1, replica_groups=mesh['dp'=8,'tensor'=4] {'dp'}, use_global_device_ids=true, to_apply=%region_9.0 | all-reduce | flops 98304 | bytes 589824 | tf_op jit(solution)/shard_map/psum | solution.py:27
  108.5 0.1 copy.21
  108.6 10.3 %all_to_all.33 = bf16[6,16,1024]{2,0,1:T(8,128)(2,1)S(1)} all-to-all(bf16[6,16,1024]{2,0,1:T(8,128)(2,1)S(1)} %copy.21), channel_id=1, replica_groups=mesh['dp'=8,'tensor'=4] {'tensor'}, dimensions={1} | all-to-all | bytes 393216 | tf_op jit(solution)/shard_map/all_to_all | solution.py:34
  118.9 0.2 copy.40
  119.1 0.2 reshape.37
  119.2 9.2 %fusion.6 = f32[6,1,4,1792]{3,0,2,1:T(8,128)S(1)} fusion(bf16[1,1792,4096]{2,1,0:T(8,128)(2,1)} %param.7, bf16[6,4,4096]{2,1,0:T(4,128)(2,1)S(1)} %reshape.37), kind=kOutput, calls=%fused_computation.8 | convolution fusion | flops 352321536 | bytes 15048704 | tf_op jit(solution)/shard_map/nksd,kfd->nksf/dot_general | solution.py:37
  128.4 9.2 %fusion.18 = bf16[6,4,1792]{2,0,1:T(8,128)(2,1)S(1)} fusion(bf16[1,1792,4096]{2,1,0:T(8,128)(2,1)} %param.8, bf16[6,4,4096]{2,1,0:T(4,128)(2,1)S(1)} %reshape.37, f32[6,1,4,1792]{3,0,2,1:T(8,128)S(1)} %fusion.6), kind=kOutput, calls=%fused_computation.12 | convolution fusion | flops 352579584 | bytes 15134720 | tf_op jit(solution)/shard_map/nksd,kfd->nksf/dot_general | solution.py:38
  137.6 7.4 %fusion = f32[6,4,4096]{2,1,0:T(4,128)S(1)} fusion(bf16[1,1792,4096]{2,1,0:T(8,128)(2,1)} %param.9, bf16[6,4,1792]{2,0,1:T(8,128)(2,1)S(1)} %fusion.18), kind=kOutput, calls=%fused_computation | convolution fusion | flops 352321536 | bytes 15159296 | tf_op jit(solution)/shard_map/nksf,kfd->nksd/dot_general | solution.py:40
  145.0 0.0 copy-start.2
  145.0 0.0 copy-start.1
  145.0 28.9 %all-reduce.6 = bf16[6,4,4096]{2,1,0:T(4,128)(2,1)S(1)} all-reduce(f32[6,4,4096]{2,1,0:T(4,128)S(1)} %fusion), channel_id=1, replica_groups=mesh['dp'=8,'tensor'=4] {'dp'}, use_global_device_ids=true, to_apply=%region_10.11 | all-reduce | flops 98304 | bytes 589824 | tf_op jit(solution)/shard_map/psum | solution.py:42
  174.0 4.8 %copy.26 = bf16[6,4,4096]{0,1,2:T(4,128)(2,1)} copy(bf16[6,4,4096]{2,1,0:T(4,128)(2,1)S(1)} %all-reduce.6) | data formatting | bytes 393216 | tf_op jit(solution)/shard_map/convert_element_type | solution.py:42
  178.7 8.1 %reshape.46 = bf16[4,2,12288]{2,1,0:T(2,128)(2,1)} reshape(bf16[4096,4,6]{2,1,0:T(4,128)(2,1)} %bitcast.60) | data formatting | bytes 393216
  186.8 3.6 %all-to-all-start.1 = ((bf16[4,2,12288]{2,1,0:T(2,128)(2,1)}), bf16[4,2,12288]{2,1,0:T(2,128)(2,1)S(1)}, u32[]{:S(2)}, u32[]{:S(2)}) async-start(bf16[4,2,12288]{2,1,0:T(2,128)(2,1)} %reshape.46), calls=%async_computation.1 | async-start | bytes 393216 | tf_op jit(solution)/shard_map/all_to_all | solution.py:43
  190.4 0.6 log_add_fusion
  191.0 5.4 %all-to-all-done.1 = bf16[4,2,12288]{2,1,0:T(2,128)(2,1)S(1)} async-done(((bf16[4,2,12288]{2,1,0:T(2,128)(2,1)}), bf16[4,2,12288]{2,1,0:T(2,128)(2,1)S(1)}, u32[]{:S(2)}, u32[]{:S(2)}) %all-to-all-start.1) | async-done | bytes 196640 | tf_op jit(solution)/shard_map/all_to_all | solution.py:43
  196.4 10.5 %reshape.47 = bf16[4096,4,6]{2,1,0:T(4,128)(2,1)} reshape(bf16[4,2,12288]{2,1,0:T(2,128)(2,1)S(1)} %all-to-all-done.1) | data formatting | bytes 393216
  206.8 6.2 %copy.28 = bf16[6,4,4,1024]{3,2,1,0:T(4,128)(2,1)S(1)} copy(bf16[6,4,4,1024]{0,2,3,1:T(4,128)(2,1)} %bitcast.61) | data formatting | bytes 393216 | tf_op jit(solution)/shard_map/all_to_all | solution.py:43
  213.0 0.1 all_to_all.30
  213.1 0.0 copy-done.2
  213.1 4.5 %convolution_convert_fusion = bf16[6,512,1024]{2,1,0:T(8,128)(2,1)} fusion(bf16[6,16,1024]{2,1,0:T(8,128)(2,1)S(1)} %all_to_all.30, f32[6,16,512]{2,1,0:T(8,128)S(1)} %copy-done.2, f32[6,512]{1,0:T(8,128)S(1)} %get-tuple-element.2, f32[6,512]{1,0:T(8,128)S(1)} %multiply_reduce_fusion.2, f32[6,512]{1,0:T(8,128)S(1)} %add_rsqrt_fusion), kind=kOutput, calls=%fused_computation.7 | convolution fusion | flops 104005632 | bytes 6721536 | tf_op jit(solution)/shard_map/gst,gsd->gtd/dot_general | solution.py:44
  217.6 0.0 copy-done.1
  (1 shorter events, 0.0 us)
Async XLA Ops:
  7.2 0.8 copy-start
  7.2 43.8 %all-reduce.4.cloned.1.call-start = ((), (), s32[]{:S(2)}) async-start(), calls=%async_computation.2 | async-start | bytes 393216 | tf_op jit(solution)/shard_map/psum | solution.py:18
  145.0 68.1 %copy-start.2 = (f32[6,16,512]{2,1,0:T(8,128)S(1)}, f32[6,16,512]{2,1,0:T(8,128)}, u32[]{:S(2)}) copy-start(f32[6,16,512]{2,1,0:T(8,128)} %all-reduce.4.cloned.1.call-done) | copy-start | bytes 589828
  145.0 72.6 %copy-start.1 = (bf16[16,1024]{1,0:T(8,128)(2,1)S(1)}, bf16[16,1024]{1,0:T(8,128)(2,1)}, u32[]{:S(2)}) copy-start(bf16[16,1024]{1,0:T(8,128)(2,1)} %param.6) | copy-start | bytes 98308
  186.8 9.6 %all-to-all-start.1 = ((bf16[4,2,12288]{2,1,0:T(2,128)(2,1)}), bf16[4,2,12288]{2,1,0:T(2,128)(2,1)S(1)}, u32[]{:S(2)}, u32[]{:S(2)}) async-start(bf16[4,2,12288]{2,1,0:T(2,128)(2,1)} %reshape.46), calls=%async_computation.1 | async-start | bytes 393216 | tf_op jit(solution)/shard_map/all_to_all | solution.py:43
Sparse Core Ops, SparseCore 0:
  13.3 37.6 all-reduce.3
where the time goes:
time: 225 us; the launch traced here: 224 us
  blocking collectives  110 us (49%)
  matrix products  39.4 us (18%)
  local copies, waits for them, and re-layouts  30.7 us (14%)
  waiting for transfers between devices  18.5 us (8%)
  between operations  14.2 us (6%)
  other arithmetic  7.83 us (3%)
  starting transfers between devices  3.62 us (2%)
    psum x1, blocking collectives, per_device(): slot_out = lax.psum(partial_out, 'dp').astype(jnp.bfloat16)  28.9 us
    psum x1, blocking collectives, per_device(): lax.psum(partial_value / column_sum[:, :, None], 'dp').astype(jnp.bfloat16)  26.8 us
    psum x1, blocking collectives, per_device(): raw_logits, squares = lax.psum((raw_logits, squares), 'tensor')  20.6 us
    unnamed x8, local copies, waits for them, and re-layouts  19.2 us
    psum x1, waiting for transfers between devices, per_device(): raw_logits, squares = lax.psum((raw_logits, squares), 'tensor')  13.1 us
    psum x1, blocking collectives, per_device(): column_sum = lax.psum(local_sum, 'dp')  11.8 us
    pmax x1, blocking collectives, per_device(): peaks = lax.pmax(jnp.max(logits, axis=2), 'dp')  11.8 us
    all_to_all x1, blocking collectives, per_device(): lax.all_to_all(slot_in, 'tensor', split_axis=1, concat_axis=2, tiled=True)  10.3 us
  transfers between devices with their start and end apart: 2, of which 2 were waited for; matrix products, arithmetic and copies ran while one was open for 2% of the time, Pallas kernels for 0%

commit v1 on v0

v1 whole, which is shorter than its diff:
```python
import functools

import jax
import jax.numpy as jnp
from jax import lax
from jax.experimental import pallas as pl
from jax.experimental.pallas import tpu as pltpu
from jax.sharding import PartitionSpec as P

SLOTS = 4
PAD = 32
LANES = 128
CHUNKS = 2
WPARTS = 4
epsilon = 1e-05
f32 = jnp.float32
bf16 = jnp.bfloat16
MESH = pl.DeviceIdType.MESH
NT = (((1,), (1,)), ((), ()))
NN = (((1,), (0,)), ((), ()))


def dispatch_kernel(
    nd, nt, tokens, router, w_gate, w_up, w_down,
    window_out, combine_out, total_out,
    tok, wg, wu, wd, stat, stat_in, logit, stats, pbuf, rbuf, abuf, zin, xin, x_all, hidden,
    obuf, oin, bbuf, zout,
    tok_sem, w_sem,
    rs_s, rs_r, ag_s, ag_r, st_s, st_r, pr_s, pr_r, az_s, az_r, ax_s, ax_r,
    or_s, or_r, bz_s, bz_r, bx_s, bx_r,
):
    me_d, me_t = lax.axis_index("dp"), lax.axis_index("tensor")
    groups, count, width = tok.shape
    owners = width // LANES
    quarter = count // nt
    per = groups // CHUNKS
    full_width = width * nt
    hidden_here = wg.shape[0]
    wrows = hidden_here // WPARTS
    is_owner_all = nd == owners

    def token_copy(g):
        return pltpu.make_async_copy(tokens.at[g], tok.at[g], tok_sem.at[g])

    def weight_copy(m, p):
        src, dst = ((w_gate, wg), (w_up, wu), (w_down, wd))[m]
        rows = pl.ds(p * wrows, wrows)
        return pltpu.make_async_copy(src.at[rows, :], dst.at[rows, :], w_sem.at[m, p])

    def ring(me, n, fn):
        def step(k, c):
            fn(lax.rem(me + k, n))
            return c
        lax.fori_loop(1, n, step, 0)

    def other_tensor(fn):
        ring(me_t, nt, fn)

    def other_dp(fn):
        ring(me_d, nd, fn)

    def other_owners(fn):
        if is_owner_all:
            ring(me_d, nd, fn)
        else:
            def step(j, c):
                pl.when(j != me_d)(functools.partial(fn, j))
                return c
            lax.fori_loop(0, owners, step, 0)

    def if_owner(fn):
        if is_owner_all:
            fn()
        else:
            pl.when(me_d < owners)(fn)

    def send(src, dst, s, r, axis, to):
        return pltpu.make_async_remote_copy(
            src_ref=src, dst_ref=dst, send_sem=s, recv_sem=r,
            device_id={axis: to}, device_id_type=MESH)

    for g in range(groups):
        token_copy(g).start()

    barrier = pltpu.get_barrier_semaphore()
    other_tensor(lambda t: pl.semaphore_signal(
        barrier, inc=1, device_id={"tensor": t}, device_id_type=MESH))
    other_dp(lambda d: pl.semaphore_signal(
        barrier, inc=1, device_id={"dp": d}, device_id_type=MESH))

    ones = jnp.ones((8, LANES), f32)
    router_rows = router[...]

    for c in range(CHUNKS):
        def partial_logits(gl, carry, c=c):
            g = c * per + gl
            token_copy(g).wait()
            raw = lax.dot_general(router_rows, tok[g], NT, preferred_element_type=f32)
            rows = pl.ds(pl.multiple_of(gl * 16, 16), 16)
            for q in range(nt):
                stat[c, q, rows, :] = raw[:, q * quarter:(q + 1) * quarter]
                acc = jnp.zeros((quarter, LANES), f32)
                for b in range(owners):
                    part = tok[g, q * quarter:(q + 1) * quarter, b * LANES:(b + 1) * LANES].astype(f32)
                    acc = acc + part * part
                sq = lax.dot_general(ones, acc, NT, precision=lax.Precision.HIGHEST,
                                     preferred_element_type=f32)
                stat[c, q, pl.ds(per * 16 + gl, 1), :] = sq[0:1]
            return carry
        stat[c, :, per * 16:, :] = jnp.zeros((nt, 8, LANES), f32)
        lax.fori_loop(0, per, partial_logits, 0)
        if c == 0:
            pl.semaphore_wait(barrier, nt - 1 + nd - 1)
        other_tensor(lambda t, c=c: send(
            stat.at[c, t], stat_in.at[c, me_t], rs_s.at[c, t], rs_r.at[c, me_t], "tensor", t).start())
        if c == 0:
            for p in range(WPARTS):
                weight_copy(0, p).start()
    for m in (1, 2):
        for p in range(WPARTS):
            weight_copy(m, p).start()

    for c in range(CHUNKS):
        stat_in[c, me_t] = stat[c, me_t]
        other_tensor(lambda t, c=c: send(
            stat.at[c, t], stat_in.at[c, t], rs_s.at[c, t], rs_r.at[c, t], "tensor", t).wait_recv())
        total = stat_in[c, 0]
        for t in range(1, nt):
            total = total + stat_in[c, t]
        norm = lax.rsqrt(total[per * 16:] / full_width + epsilon)
        for gl in range(per):
            logit[c, me_t, gl * 16:(gl + 1) * 16, :] = total[gl * 16:(gl + 1) * 16] * norm[gl:gl + 1]
        logit[c, me_t, per * 16:, :] = norm
        other_tensor(lambda t, c=c: send(
            logit.at[c, me_t], logit.at[c, me_t], ag_s.at[c, t], ag_r.at[c, me_t], "tensor", t).start())

    stats[me_d] = jnp.ones(stats.shape[1:], f32)
    column = lax.broadcasted_iota(jnp.int32, (16, LANES), 1)
    for c in range(CHUNKS):
        other_tensor(lambda t, c=c: send(
            logit.at[c, t], logit.at[c, t], ag_s.at[c, t], ag_r.at[c, t], "tensor", t).wait_recv())

        def weigh(gl, carry, c=c):
            g = c * per + gl
            rows = pl.ds(pl.multiple_of(gl * 16, 16), 16)
            logits = jnp.concatenate([logit[c, q, rows, :] for q in range(nt)], axis=1)
            norm = jnp.concatenate([logit[c, q, pl.ds(per * 16 + gl, 1), :] for q in range(nt)], axis=1)
            peak = jnp.max(logits, axis=1, keepdims=True)
            powers = jnp.exp(logits - peak)
            csum = jnp.sum(powers, axis=1, keepdims=True)
            weights = (powers * norm).astype(bf16)
            summed = lax.dot_general(weights, tok[g], NN, preferred_element_type=f32)
            for j in range(owners):
                pbuf[c, j, gl] = summed[:, j * LANES:(j + 1) * LANES].astype(bf16)
            stats[me_d, 0] = jnp.where(column == g, peak, stats[me_d, 0])
            stats[me_d, 1] = jnp.where(column == g, csum, stats[me_d, 1])
            return carry
        lax.fori_loop(0, per, weigh, 0)
        if c == CHUNKS - 1:
            other_owners(lambda j: send(
                stats.at[me_d], stats.at[me_d], st_s.at[j], st_r.at[me_d], "dp", j).start())
        other_owners(lambda j, c=c: send(
            pbuf.at[c, j], rbuf.at[c, me_d], pr_s.at[c, j], pr_r.at[c, me_d], "dp", j).start())

    for c in range(CHUNKS):
        def mixing(gl, carry, c=c):
            g = c * per + gl
            rows = pl.ds(pl.multiple_of(gl * 16, 16), 16)
            logits = jnp.concatenate([logit[c, q, rows, :] for q in range(nt)], axis=1)
            row_peak = jnp.max(logits, axis=0, keepdims=True)
            row_powers = jnp.exp(logits - row_peak)
            row_sum = jnp.sum(row_powers, axis=0, keepdims=True)
            combine_out[g] = (row_powers / row_sum).astype(bf16)
            total_out[pl.ds(g, 1), :] = row_peak + jnp.log(row_sum)
            return carry
        lax.fori_loop(0, per, mixing, 0)

    def spread_matrix(rows, cols, flip):
        a = lax.broadcasted_iota(jnp.int32, (rows, cols), 1 if flip else 0)
        b = lax.broadcasted_iota(jnp.int32, (rows, cols), 0 if flip else 1)
        k, q = a // PAD, a % PAD
        source = (q // SLOTS) * 16 + k * SLOTS + q % SLOTS
        hit = jnp.logical_and(q < groups * SLOTS, source == b)
        return jnp.where(hit, 1.0, 0.0).astype(bf16)

    spread = spread_matrix(nt * PAD, groups * 16, False)
    gather = spread_matrix(groups * 16, nt * PAD, True)

    def reduce_slots():
        for c in range(CHUNKS):
            other_dp(lambda d, c=c: send(
                pbuf.at[c, 0], rbuf.at[c, d], pr_s.at[c, 0], pr_r.at[c, d], "dp", d).wait_recv())
            rbuf[c, me_d] = pbuf[c, me_d]
        other_dp(lambda d: send(
            stats.at[d], stats.at[d], st_s.at[0], st_r.at[d], "dp", d).wait_recv())
        peak = stats[0, 0]
        for i in range(1, nd):
            peak = jnp.maximum(peak, stats[i, 0])
        factor = [jnp.exp(stats[i, 0] - peak) for i in range(nd)]
        den = factor[0] * stats[0, 1]
        for i in range(1, nd):
            den = den + factor[i] * stats[i, 1]
        scale = [f / den for f in factor]
        rows = []
        for g in range(groups):
            c, gl = g // per, g % per
            acc = jnp.zeros((16, LANES), f32)
            for i in range(nd):
                acc = acc + scale[i][:, g:g + 1] * rbuf[c, i, gl].astype(f32)
            rows.append(acc.astype(bf16))
        slot_in = jnp.concatenate(rows, axis=0)
        moved = lax.dot_general(spread, slot_in, NN, preferred_element_type=f32).astype(bf16)
        for k in range(nt):
            abuf[k] = moved[k * PAD:(k + 1) * PAD]
        zin[me_t] = abuf[me_t]
        other_tensor(lambda t: send(
            abuf.at[t], zin.at[me_t], az_s.at[t], az_r.at[me_t], "tensor", t).start())
        other_tensor(lambda t: send(
            abuf.at[t], zin.at[t], az_s.at[t], az_r.at[t], "tensor", t).wait_recv())
        xin[me_d] = zin[...]
        other_dp(lambda d: send(
            zin, xin.at[me_d], ax_s.at[d], ax_r.at[me_d], "dp", d).start())
    if_owner(reduce_slots)
    other_owners(lambda j: send(
        zin, xin.at[j], ax_s.at[0], ax_r.at[j], "dp", j).wait_recv())

    for i in range(owners):
        for t in range(nt):
            x_all[:, t * width + i * LANES:t * width + (i + 1) * LANES] = xin[i, t]

    for m in (0, 1):
        for p in range(WPARTS):
            weight_copy(m, p).wait()
    fc = 256 if hidden_here % 256 == 0 else hidden_here

    def hidden_part(f, carry):
        at = pl.multiple_of(f * fc, fc)
        rows = pl.ds(at, fc)
        x = x_all[...]
        gate = lax.dot_general(x, wg[rows, :], NT, preferred_element_type=f32)
        up = lax.dot_general(x, wu[rows, :], NT, preferred_element_type=f32)
        act = gate / (1.0 + jnp.exp(-gate)) * up
        hidden[:, pl.ds(at, fc)] = act.astype(bf16)
        return carry
    lax.fori_loop(0, hidden_here // fc, hidden_part, 0)

    for p in range(WPARTS):
        weight_copy(2, p).wait()

    pairs = owners // 2

    def down_part(k, carry):
        p = lax.rem(k + me_d // 2 + 1, pairs)
        for t in range(nt):
            cols = pl.ds(pl.multiple_of(t * width + p * 2 * LANES, 2 * LANES), 2 * LANES)
            out = lax.dot_general(hidden[...], wd[:, cols], NN, preferred_element_type=f32)
            obuf[2 * p, t] = out[:, :LANES].astype(bf16)
            obuf[2 * p + 1, t] = out[:, LANES:].astype(bf16)
        for h in range(2):
            j = 2 * p + h

            @pl.when(j != me_d)
            def _():
                send(obuf.at[j], oin.at[me_d], or_s.at[j], or_r.at[me_d], "dp", j).start()
        return carry
    lax.fori_loop(0, pairs, down_part, 0)

    def reduce_outputs():
        oin[me_d] = obuf[me_d]
        other_dp(lambda d: send(
            obuf.at[0], oin.at[d], or_s.at[0], or_r.at[d], "dp", d).wait_recv())
        for t in range(nt):
            acc = oin[0, t].astype(f32)
            for i in range(1, nd):
                acc = acc + oin[i, t].astype(f32)
            bbuf[t] = acc.astype(bf16)
        zout[me_t] = bbuf[me_t]
        other_tensor(lambda t: send(
            bbuf.at[t], zout.at[me_t], bz_s.at[t], bz_r.at[me_t], "tensor", t).start())
        other_tensor(lambda t: send(
            bbuf.at[t], zout.at[t], bz_s.at[t], bz_r.at[t], "tensor", t).wait_recv())
        rows = jnp.concatenate([zout[k] for k in range(nt)], axis=0)
        window_out[me_d] = lax.dot_general(
            gather, rows, NN, preferred_element_type=f32).astype(bf16)
        other_dp(lambda d: send(
            window_out.at[me_d], window_out.at[me_d], bx_s.at[d], bx_r.at[me_d], "dp", d).start())
    if_owner(reduce_outputs)
    other_owners(lambda j: send(
        window_out.at[j], window_out.at[j], bx_s.at[0], bx_r.at[j], "dp", j).wait_recv())

    for c in range(CHUNKS):
        other_tensor(lambda t, c=c: send(
            stat.at[c, t], stat_in.at[c, t], rs_s.at[c, t], rs_r.at[c, t], "tensor", t).wait_send())
        other_tensor(lambda t, c=c: send(
            logit.at[c, me_t], logit.at[c, me_t], ag_s.at[c, t], ag_r.at[c, t], "tensor", t).wait_send())
        other_owners(lambda j, c=c: send(
            pbuf.at[c, j], rbuf.at[c, j], pr_s.at[c, j], pr_r.at[c, j], "dp", j).wait_send())
    other_owners(lambda j: send(
        stats.at[me_d], stats.at[me_d], st_s.at[j], st_r.at[j], "dp", j).wait_send())
    other_owners(lambda j: send(
        obuf.at[j], oin.at[j], or_s.at[j], or_r.at[j], "dp", j).wait_send())

    def drain():
        other_tensor(lambda t: send(
            abuf.at[t], zin.at[t], az_s.at[t], az_r.at[t], "tensor", t).wait_send())
        other_tensor(lambda t: send(
            bbuf.at[t], zout.at[t], bz_s.at[t], bz_r.at[t], "tensor", t).wait_send())
        other_dp(lambda d: send(
            zin, xin.at[0], ax_s.at[d], ax_r.at[d], "dp", d).wait_send())
        other_dp(lambda d: send(
            window_out.at[me_d], window_out.at[me_d], bx_s.at[d], bx_r.at[d], "dp", d).wait_send())
    if_owner(drain)


def mix_kernel(combine, window, total, mixed, total_out):
    slots = jnp.concatenate([window[j, 0] for j in range(window.shape[0])], axis=1)
    mixed[0] = lax.dot_general(
        combine[0], slots, (((0,), (0,)), ((), ())), preferred_element_type=f32).astype(bf16)
    total_out[...] = total[...]


def per_device(tokens, router, w_gate, w_up, w_down):
    nd, nt = lax.axis_size("dp"), lax.axis_size("tensor")
    groups, count, width = tokens.shape
    hidden_here, full = w_gate.shape[1:]
    slots = router.shape[0]
    owners = width // LANES
    quarter = count // nt
    per = groups // CHUNKS
    srows = per * 16 + 8
    VM, DMA = pltpu.VMEM, pltpu.SemaphoreType.DMA
    any_spec = pl.BlockSpec(memory_space=pl.ANY)
    vmem_spec = pl.BlockSpec(memory_space=pltpu.VMEM)
    window, combine, total = pl.pallas_call(
        functools.partial(dispatch_kernel, nd, nt),
        out_shape=(
            jax.ShapeDtypeStruct((owners, groups * slots, LANES), bf16),
            jax.ShapeDtypeStruct((groups, slots, count), bf16),
            jax.ShapeDtypeStruct((groups, count), f32),
        ),
        in_specs=[any_spec, vmem_spec, any_spec, any_spec, any_spec],
        out_specs=(vmem_spec, vmem_spec, vmem_spec),
        scratch_shapes=[
            VM((groups, count, width), bf16),
            VM((hidden_here, full), bf16),
            VM((hidden_here, full), bf16),
            VM((hidden_here, full), bf16),
            VM((CHUNKS, nt, srows, quarter), f32),
            VM((CHUNKS, nt, srows, quarter), f32),
            VM((CHUNKS, nt, srows, quarter), f32),
            VM((nd, 2, slots, LANES), f32),
            VM((CHUNKS, owners, per, slots, LANES), bf16),
            VM((CHUNKS, nd, per, slots, LANES), bf16),
            VM((nt, PAD, LANES), bf16),
            VM((nt, PAD, LANES), bf16),
            VM((owners, nt, PAD, LANES), bf16),
            VM((PAD, full), bf16),
            VM((PAD, hidden_here), bf16),
            VM((owners, nt, PAD, LANES), bf16),
            VM((nd, nt, PAD, LANES), bf16),
            VM((nt, PAD, LANES), bf16),
            VM((nt, PAD, LANES), bf16),
            DMA((groups,)), DMA((3, WPARTS)),
            DMA((CHUNKS, nt)), DMA((CHUNKS, nt)), DMA((CHUNKS, nt)), DMA((CHUNKS, nt)),
            DMA((owners,)), DMA((nd,)), DMA((CHUNKS, owners)), DMA((CHUNKS, nd)),
            DMA((nt,)), DMA((nt,)), DMA((nd,)), DMA((owners,)),
            DMA((owners,)), DMA((nd,)), DMA((nt,)), DMA((nt,)), DMA((nd,)), DMA((owners,)),
        ],
        compiler_params=pltpu.CompilerParams(
            collective_id=0, has_side_effects=True, vmem_limit_bytes=58 * 1024 * 1024),
        name="dispatch",
    )(tokens, router, w_gate[0], w_up[0], w_down[0])
    window = window.reshape(owners, groups, slots, LANES)
    mixed, log_total = pl.pallas_call(
        mix_kernel,
        grid=(groups,),
        out_shape=(
            jax.ShapeDtypeStruct((groups, count, width), bf16),
            jax.ShapeDtypeStruct((groups, count), f32),
        ),
        in_specs=[
            pl.BlockSpec((1, slots, count), lambda g: (g, 0, 0)),
            pl.BlockSpec((owners, 1, slots, LANES), lambda g: (0, g, 0, 0)),
            pl.BlockSpec((groups, count), lambda g: (0, 0)),
        ],
        out_specs=(
            pl.BlockSpec((1, count, width), lambda g: (g, 0, 0)),
            pl.BlockSpec((groups, count), lambda g: (0, 0)),
        ),
        name="mix",
    )(combine, window, total)
    return (mixed, log_total)


def solution(mesh):
    in_specs = (
        P(None, "dp", "tensor"),
        P(None, "tensor"),
        P("tensor", "dp", None),
        P("tensor", "dp", None),
        P("tensor", "dp", None),
    )
    out_specs = (P(None, "dp", "tensor"), P(None, "dp"))
    return jax.shard_map(
        per_device, mesh=mesh, in_specs=in_specs, out_specs=out_specs, check_vma=False
    )
```

time: 225 us -> 65.3 us (0.29)
  blocking collectives: 110 us -> 0 us
  Pallas kernels: 0 us -> 64.2 us
  matrix products: 39.4 us -> 0 us
  local copies, waits for them, and re-layouts: 30.7 us -> 0 us
  waiting for transfers between devices: 18.5 us -> 0 us
  between operations: 14.2 us -> 0.64 us
  other arithmetic: 7.83 us -> 0 us
  starting transfers between devices: 3.62 us -> 0 us
    psum x4 -> x0, blocking collectives: 88.2 us -> none  [the longest x1 28.9 us: per_device(): slot_out = lax.psum(partial_out, 'dp').astype(jnp.bfloat16)]
    pallas_call x0 -> x2, Pallas kernels: none -> 64.2 us  [the longest x1 58.3 us: per_device(): pl.pallas_call(functools.partial(dispatch_kernel, nd, nt), out_shape=(jax...]
    dot_general x6 -> x0, matrix products: 39.4 us -> none  [the longest x1 9.19 us: per_device(): jnp.einsum('nksd,kfd->nksf', grouped, w_gate, preferred_element_type=jnp....]
    unnamed x8 -> x0, local copies, waits for them, and re-layouts: 19.2 us -> none
    psum x1 -> x0, waiting for transfers between devices: 13.1 us -> none  [per_device(): raw_logits, squares = lax.psum((raw_logits, squares), 'tensor')]
    pmax x1 -> x0, blocking collectives: 11.8 us -> none  [per_device(): peaks = lax.pmax(jnp.max(logits, axis=2), 'dp')]
    all_to_all x1 -> x0, blocking collectives: 10.3 us -> none  [per_device(): lax.all_to_all(slot_in, 'tensor', split_axis=1, concat_axis=2, tiled=True)]
    all_to_all x3 -> x0, local copies, waits for them, and re-layouts: 6.36 us -> none  [the longest x2 6.21 us: per_device(): lax.all_to_all(slot_out, 'tensor', split_axis=2, concat_axis=1, tiled=True)]
  transfers between devices with their start and end apart: 2 -> 0, of which waited for: 2 -> 0; matrix products, arithmetic and copies ran while one was open for 2% -> 0% of each run, Pallas kernels for 0% -> 0%
where the time goes in v1:
time: 65.3 us; the launch traced here: 64.8 us
  Pallas kernels  64.2 us (98%)
    pallas_call x1, Pallas kernels, per_device(): pl.pallas_call(functools.partial(dispatch_kernel, nd, nt), out_shape=(jax...  58.3 us
    pallas_call x1, Pallas kernels, per_device(): pl.pallas_call(mix_kernel, grid=(groups,), out_shape=(jax.ShapeDtypeStruc...  5.94 us

profile of v1, /device:TPU:0, one launch (start us, length us, event | category | flops | bytes accessed | tf_op | source)
XLA Modules:
  0.0 64.8 jit_solution(17978463207515627105)
XLA Ops:
  0.6 58.3 %dispatch.1 = (bf16[8,96,128]{2,1,0:T(8,128)(2,1)}, bf16[6,16,512]{2,1,0:T(8,128)(2,1)}, f32[6,512]{1,0:T(8,128)}) custom-call(bf16[6,512,1024]{2,1,0:T(8,128)(2,1)} %tokens.1, bf16[16,1024]{1,0:T(8,128)(2,1)} %router.1, bf16[1792,4096]{1,0:T(8,128)(2,1)} %bitcast.4, bf16[1792,4096]{1,0:T(8,128)(2,1)} %bitcast.5, bf16[1792,4096]{1,0:T(8,128)(2,1)} %bitcast.6), custom_call_target="tpu_custom_call" | custom-call | tf_op jit(solution)/shard_map/dispatch/pallas_call | solution.py:334
  58.9 5.9 %mix.1 = (bf16[6,512,1024]{2,1,0:T(8,128)(2,1)}, f32[6,512]{1,0:T(8,128)}) custom-call(bf16[6,16,512]{2,1,0:T(8,128)(2,1)} %get-tuple-element.5.combine, bf16[8,6,16,128]{3,2,1,0:T(8,128)(2,1)} %bitcast.7, f32[6,512]{1,0:T(8,128)} %get-tuple-element.7.total), custom_call_target="tpu_custom_call" | custom-call | tf_op jit(solution)/shard_map/mix/pallas_call | solution.py:374

commit v2 on v1

--- a/solution.py
+++ b/solution.py
@@ -23,10 +23,10 @@
 def dispatch_kernel(
     nd, nt, tokens, router, w_gate, w_up, w_down,
     window_out, combine_out, total_out,
-    tok, wg, wu, wd, stat, stat_in, logit, stats, pbuf, rbuf, abuf, zin, xin, x_all, hidden,
+    tok, wg, wu, wd, stat, stat_in, wbuf, sbuf, stats, pbuf, rbuf, abuf, zin, xin, x_all, hidden,
     obuf, oin, bbuf, zout,
     tok_sem, w_sem,
-    rs_s, rs_r, ag_s, ag_r, st_s, st_r, pr_s, pr_r, az_s, az_r, ax_s, ax_r,
+    rs_s, rs_r, ag_s, ag_r, as_s, as_r, cb_s, cb_r, tb_s, tb_r, st_s, st_r, pr_s, pr_r, az_s, az_r, ax_s, ax_r,
     or_s, or_r, bz_s, bz_r, bx_s, bx_r,
 ):
     me_d, me_t = lax.axis_index("dp"), lax.axis_index("tensor")
@@ -88,7 +88,6 @@
     other_dp(lambda d: pl.semaphore_signal(
         barrier, inc=1, device_id={"dp": d}, device_id_type=MESH))
 
-    ones = jnp.ones((8, LANES), f32)
     router_rows = router[...]
 
     for c in range(CHUNKS):
@@ -103,9 +102,7 @@
                 for b in range(owners):
                     part = tok[g, q * quarter:(q + 1) * quarter, b * LANES:(b + 1) * LANES].astype(f32)
                     acc = acc + part * part
-                sq = lax.dot_general(ones, acc, NT, precision=lax.Precision.HIGHEST,
-                                     preferred_element_type=f32)
-                stat[c, q, pl.ds(per * 16 + gl, 1), :] = sq[0:1]
+                stat[c, q, pl.ds(per * 16 + gl, 1), :] = jnp.sum(acc.T, axis=0, keepdims=True)
             return carry
         stat[c, :, per * 16:, :] = jnp.zeros((nt, 8, LANES), f32)
         lax.fori_loop(0, per, partial_logits, 0)
@@ -120,6 +117,9 @@
         for p in range(WPARTS):
             weight_copy(m, p).start()
 
+    column = lax.broadcasted_iota(jnp.int32, (16, LANES), 1)
+    half = LANES // 2
+    total_out[me_t] = jnp.zeros(total_out.shape[1:], f32)
     for c in range(CHUNKS):
         stat_in[c, me_t] = stat[c, me_t]
         other_tensor(lambda t, c=c: send(
@@ -128,52 +128,69 @@
         for t in range(1, nt):
             total = total + stat_in[c, t]
         norm = lax.rsqrt(total[per * 16:] / full_width + epsilon)
+        summary = jnp.zeros((16, LANES), f32)
+        all_logits = []
         for gl in range(per):
-            logit[c, me_t, gl * 16:(gl + 1) * 16, :] = total[gl * 16:(gl + 1) * 16] * norm[gl:gl + 1]
-        logit[c, me_t, per * 16:, :] = norm
-        other_tensor(lambda t, c=c: send(
-            logit.at[c, me_t], logit.at[c, me_t], ag_s.at[c, t], ag_r.at[c, me_t], "tensor", t).start())
-
-    stats[me_d] = jnp.ones(stats.shape[1:], f32)
-    column = lax.broadcasted_iota(jnp.int32, (16, LANES), 1)
-    for c in range(CHUNKS):
-        other_tensor(lambda t, c=c: send(
-            logit.at[c, t], logit.at[c, t], ag_s.at[c, t], ag_r.at[c, t], "tensor", t).wait_recv())
-
-        def weigh(gl, carry, c=c):
             g = c * per + gl
-            rows = pl.ds(pl.multiple_of(gl * 16, 16), 16)
-            logits = jnp.concatenate([logit[c, q, rows, :] for q in range(nt)], axis=1)
-            norm = jnp.concatenate([logit[c, q, pl.ds(per * 16 + gl, 1), :] for q in range(nt)], axis=1)
+            logits = total[gl * 16:(gl + 1) * 16] * norm[gl:gl + 1]
+            all_logits.append(logits)
             peak = jnp.max(logits, axis=1, keepdims=True)
             powers = jnp.exp(logits - peak)
             csum = jnp.sum(powers, axis=1, keepdims=True)
-            weights = (powers * norm).astype(bf16)
-            summed = lax.dot_general(weights, tok[g], NN, preferred_element_type=f32)
+            wbuf[c, me_t, gl] = (powers * norm[gl:gl + 1]).astype(bf16)
+            summary = jnp.where(column == g, peak, jnp.where(column == half + g, csum, summary))
+        sbuf[c, me_t] = summary
+        other_tensor(lambda t, c=c: send(
+            sbuf.at[c, me_t], sbuf.at[c, me_t], as_s.at[c, t], as_r.at[c, me_t], "tensor", t).start())
+        other_tensor(lambda t, c=c: send(
+            wbuf.at[c, me_t], wbuf.at[c, me_t], ag_s.at[c, t], ag_r.at[c, me_t], "tensor", t).start())
+        for gl in range(per):
+            g = c * per + gl
+            logits = all_logits[gl]
+            row_peak = jnp.max(logits, axis=0, keepdims=True)
+            row_powers = jnp.exp(logits - row_peak)
+            row_sum = jnp.sum(row_powers, axis=0, keepdims=True)
+            combine_out[me_t, g] = (row_powers / row_sum).astype(bf16)
+            total_out[me_t, g:g + 1, :] = row_peak + jnp.log(row_sum)
+
+    for c in range(CHUNKS):
+        other_tensor(lambda t, c=c: send(
+            sbuf.at[c, t], sbuf.at[c, t], as_s.at[c, t], as_r.at[c, t], "tensor", t).wait_recv())
+        peak = sbuf[c, 0]
+        for q in range(1, nt):
+            peak = jnp.maximum(peak, sbuf[c, q])
+        factor = [jnp.exp(sbuf[c, q] - peak) for q in range(nt)]
+        csum = factor[0] * pltpu.roll(sbuf[c, 0], half, 1)
+        for q in range(1, nt):
+            csum = csum + factor[q] * pltpu.roll(sbuf[c, q], half, 1)
+        mine = jnp.logical_and(column >= c * per, column < (c + 1) * per)
+        if c == 0:
+            stats[me_d, 0] = jnp.where(mine, peak, 0.0)
+            stats[me_d, 1] = jnp.where(mine, csum, 1.0)
+        else:
+            stats[me_d, 0] = jnp.where(mine, peak, stats[me_d, 0])
+            stats[me_d, 1] = jnp.where(mine, csum, stats[me_d, 1])
+        other_tensor(lambda t, c=c: send(
+            wbuf.at[c, t], wbuf.at[c, t], ag_s.at[c, t], ag_r.at[c, t], "tensor", t).wait_recv())
+        for gl in range(per):
+            g = c * per + gl
+            summed = jnp.zeros((16, width), f32)
+            for q in range(nt):
+                summed = summed + factor[q][:, g:g + 1] * lax.dot_general(
+                    wbuf[c, q, gl], tok[g, q * quarter:(q + 1) * quarter, :], NN,
+                    preferred_element_type=f32)
             for j in range(owners):
                 pbuf[c, j, gl] = summed[:, j * LANES:(j + 1) * LANES].astype(bf16)
-            stats[me_d, 0] = jnp.where(column == g, peak, stats[me_d, 0])
-            stats[me_d, 1] = jnp.where(column == g, csum, stats[me_d, 1])
-            return carry
-        lax.fori_loop(0, per, weigh, 0)
         if c == CHUNKS - 1:
             other_owners(lambda j: send(
                 stats.at[me_d], stats.at[me_d], st_s.at[j], st_r.at[me_d], "dp", j).start())
         other_owners(lambda j, c=c: send(
             pbuf.at[c, j], rbuf.at[c, me_d], pr_s.at[c, j], pr_r.at[c, me_d], "dp", j).start())
 
-    for c in range(CHUNKS):
-        def mixing(gl, carry, c=c):
-            g = c * per + gl
-            rows = pl.ds(pl.multiple_of(gl * 16, 16), 16)
-            logits = jnp.concatenate([logit[c, q, rows, :] for q in range(nt)], axis=1)
-            row_peak = jnp.max(logits, axis=0, keepdims=True)
-            row_powers = jnp.exp(logits - row_peak)
-            row_sum = jnp.sum(row_powers, axis=0, keepdims=True)
-            combine_out[g] = (row_powers / row_sum).astype(bf16)
-            total_out[pl.ds(g, 1), :] = row_peak + jnp.log(row_sum)
-            return carry
-        lax.fori_loop(0, per, mixing, 0)
+    other_tensor(lambda t: send(
+        combine_out.at[me_t], combine_out.at[me_t], cb_s.at[t], cb_r.at[me_t], "tensor", t).start())
+    other_tensor(lambda t: send(
+        total_out.at[me_t], total_out.at[me_t], tb_s.at[t], tb_r.at[me_t], "tensor", t).start())
 
     def spread_matrix(rows, cols, flip):
         a = lax.broadcasted_iota(jnp.int32, (rows, cols), 1 if flip else 0)
@@ -221,6 +238,21 @@
         other_dp(lambda d: send(
             zin, xin.at[me_d], ax_s.at[d], ax_r.at[me_d], "dp", d).start())
     if_owner(reduce_slots)
+    for c in range(CHUNKS):
+        other_tensor(lambda t, c=c: send(
+            stat.at[c, t], stat_in.at[c, t], rs_s.at[c, t], rs_r.at[c, t], "tensor", t).wait_send())
+        other_tensor(lambda t, c=c: send(
+            wbuf.at[c, me_t], wbuf.at[c, me_t], ag_s.at[c, t], ag_r.at[c, t], "tensor", t).wait_send())
+        other_tensor(lambda t, c=c: send(
+            sbuf.at[c, me_t], sbuf.at[c, me_t], as_s.at[c, t], as_r.at[c, t], "tensor", t).wait_send())
+        other_owners(lambda j, c=c: send(
+            pbuf.at[c, j], rbuf.at[c, j], pr_s.at[c, j], pr_r.at[c, j], "dp", j).wait_send())
+    other_owners(lambda j: send(
+        stats.at[me_d], stats.at[me_d], st_s.at[j], st_r.at[j], "dp", j).wait_send())
+    other_tensor(lambda t: send(
+        combine_out.at[me_t], combine_out.at[t], cb_s.at[t], cb_r.at[t], "tensor", t).wait_send())
+    other_tensor(lambda t: send(
+        total_out.at[me_t], total_out.at[t], tb_s.at[t], tb_r.at[t], "tensor", t).wait_send())
     other_owners(lambda j: send(
         zin, xin.at[j], ax_s.at[0], ax_r.at[j], "dp", j).wait_recv())
 
@@ -233,16 +265,12 @@
             weight_copy(m, p).wait()
     fc = 256 if hidden_here % 256 == 0 else hidden_here
 
-    def hidden_part(f, carry):
-        at = pl.multiple_of(f * fc, fc)
-        rows = pl.ds(at, fc)
+    for f in range(hidden_here // fc):
         x = x_all[...]
-        gate = lax.dot_general(x, wg[rows, :], NT, preferred_element_type=f32)
-        up = lax.dot_general(x, wu[rows, :], NT, preferred_element_type=f32)
+        gate = lax.dot_general(x, wg[f * fc:(f + 1) * fc, :], NT, preferred_element_type=f32)
+        up = lax.dot_general(x, wu[f * fc:(f + 1) * fc, :], NT, preferred_element_type=f32)
         act = gate / (1.0 + jnp.exp(-gate)) * up
-        hidden[:, pl.ds(at, fc)] = act.astype(bf16)
-        return carry
-    lax.fori_loop(0, hidden_here // fc, hidden_part, 0)
+        hidden[:, f * fc:(f + 1) * fc] = act.astype(bf16)
 
     for p in range(WPARTS):
         weight_copy(2, p).wait()
@@ -265,6 +293,17 @@
         return carry
     lax.fori_loop(0, pairs, down_part, 0)
 
+    def drain_inputs():
+        other_tensor(lambda t: send(
+            abuf.at[t], zin.at[t], az_s.at[t], az_r.at[t], "tensor", t).wait_send())
+        other_dp(lambda d: send(
+            zin, xin.at[0], ax_s.at[d], ax_r.at[d], "dp", d).wait_send())
+    if_owner(drain_inputs)
+    other_tensor(lambda t: send(
+        combine_out.at[t], combine_out.at[t], cb_s.at[t], cb_r.at[t], "tensor", t).wait_recv())
+    other_tensor(lambda t: send(
+        total_out.at[t], total_out.at[t], tb_s.at[t], tb_r.at[t], "tensor", t).wait_recv())
+
     def reduce_outputs():
         oin[me_d] = obuf[me_d]
         other_dp(lambda d: send(
@@ -288,35 +327,35 @@
     other_owners(lambda j: send(
         window_out.at[j], window_out.at[j], bx_s.at[0], bx_r.at[j], "dp", j).wait_recv())
 
-    for c in range(CHUNKS):
-        other_tensor(lambda t, c=c: send(
-            stat.at[c, t], stat_in.at[c, t], rs_s.at[c, t], rs_r.at[c, t], "tensor", t).wait_send())
-        other_tensor(lambda t, c=c: send(
-            logit.at[c, me_t], logit.at[c, me_t], ag_s.at[c, t], ag_r.at[c, t], "tensor", t).wait_send())
-        other_owners(lambda j, c=c: send(
-            pbuf.at[c, j], rbuf.at[c, j], pr_s.at[c, j], pr_r.at[c, j], "dp", j).wait_send())
-    other_owners(lambda j: send(
-        stats.at[me_d], stats.at[me_d], st_s.at[j], st_r.at[j], "dp", j).wait_send())
     other_owners(lambda j: send(
         obuf.at[j], oin.at[j], or_s.at[j], or_r.at[j], "dp", j).wait_send())
 
     def drain():
         other_tensor(lambda t: send(
-            abuf.at[t], zin.at[t], az_s.at[t], az_r.at[t], "tensor", t).wait_send())
-        other_tensor(lambda t: send(
             bbuf.at[t], zout.at[t], bz_s.at[t], bz_r.at[t], "tensor", t).wait_send())
-        other_dp(lambda d: send(
-            zin, xin.at[0], ax_s.at[d], ax_r.at[d], "dp", d).wait_send())
         other_dp(lambda d: send(
             window_out.at[me_d], window_out.at[me_d], bx_s.at[d], bx_r.at[d], "dp", d).wait_send())
     if_owner(drain)
 
 
-def mix_kernel(combine, window, total, mixed, total_out):
-    slots = jnp.concatenate([window[j, 0] for j in range(window.shape[0])], axis=1)
-    mixed[0] = lax.dot_general(
-        combine[0], slots, (((0,), (0,)), ((), ())), preferred_element_type=f32).astype(bf16)
-    total_out[...] = total[...]
+def mix_kernel(combine, window, total, mixed, total_out, held, sem):
+    nt, groups = combine.shape[:2]
+    owners, quarter = window.shape[0], combine.shape[3]
+
+    def copy(g):
+        return pltpu.make_async_copy(held.at[g], mixed.at[g], sem.at[g])
+
+    for g in range(groups):
+        slots = jnp.concatenate([window[j, g] for j in range(owners)], axis=1)
+        for q in range(nt):
+            held[g, q * quarter:(q + 1) * quarter, :] = lax.dot_general(
+                combine[q, g], slots, (((0,), (0,)), ((), ())),
+                preferred_element_type=f32).astype(bf16)
+        copy(g).start()
+    for q in range(nt):
+        total_out[:, q * quarter:(q + 1) * quarter] = total[q, :groups, :]
+    for g in range(groups):
+        copy(g).wait()
 
 
 def per_device(tokens, router, w_gate, w_up, w_down):
@@ -335,8 +374,8 @@
         functools.partial(dispatch_kernel, nd, nt),
         out_shape=(
             jax.ShapeDtypeStruct((owners, groups * slots, LANES), bf16),
-            jax.ShapeDtypeStruct((groups, slots, count), bf16),
-            jax.ShapeDtypeStruct((groups, count), f32),
+            jax.ShapeDtypeStruct((nt, groups, slots, quarter), bf16),
+            jax.ShapeDtypeStruct((nt, 8, quarter), f32),
         ),
         in_specs=[any_spec, vmem_spec, any_spec, any_spec, any_spec],
         out_specs=(vmem_spec, vmem_spec, vmem_spec),
@@ -347,7 +386,8 @@
             VM((hidden_here, full), bf16),
             VM((CHUNKS, nt, srows, quarter), f32),
             VM((CHUNKS, nt, srows, quarter), f32),
-            VM((CHUNKS, nt, srows, quarter), f32),
+            VM((CHUNKS, nt, per, slots, quarter), bf16),
+            VM((CHUNKS, nt, slots, LANES), f32),
             VM((nd, 2, slots, LANES), f32),
             VM((CHUNKS, owners, per, slots, LANES), bf16),
             VM((CHUNKS, nd, per, slots, LANES), bf16),
@@ -362,6 +402,7 @@
             VM((nt, PAD, LANES), bf16),
             DMA((groups,)), DMA((3, WPARTS)),
             DMA((CHUNKS, nt)), DMA((CHUNKS, nt)), DMA((CHUNKS, nt)), DMA((CHUNKS, nt)),
+            DMA((CHUNKS, nt)), DMA((CHUNKS, nt)), DMA((nt,)), DMA((nt,)), DMA((nt,)), DMA((nt,)),
             DMA((owners,)), DMA((nd,)), DMA((CHUNKS, owners)), DMA((CHUNKS, nd)),
             DMA((nt,)), DMA((nt,)), DMA((nd,)), DMA((owners,)),
             DMA((owners,)), DMA((nd,)), DMA((nt,)), DMA((nt,)), DMA((nd,)), DMA((owners,)),
@@ -373,20 +414,14 @@
     window = window.reshape(owners, groups, slots, LANES)
     mixed, log_total = pl.pallas_call(
         mix_kernel,
-        grid=(groups,),
         out_shape=(
             jax.ShapeDtypeStruct((groups, count, width), bf16),
             jax.ShapeDtypeStruct((groups, count), f32),
         ),
-        in_specs=[
-            pl.BlockSpec((1, slots, count), lambda g: (g, 0, 0)),
-            pl.BlockSpec((owners, 1, slots, LANES), lambda g: (0, g, 0, 0)),
-            pl.BlockSpec((groups, count), lambda g: (0, 0)),
-        ],
-        out_specs=(
-            pl.BlockSpec((1, count, width), lambda g: (g, 0, 0)),
-            pl.BlockSpec((groups, count), lambda g: (0, 0)),
-        ),
+        in_specs=[vmem_spec, vmem_spec, vmem_spec],
+        out_specs=(any_spec, vmem_spec),
+        scratch_shapes=[VM((groups, count, width), bf16), DMA((groups,))],
+        compiler_params=pltpu.CompilerParams(vmem_limit_bytes=32 * 1024 * 1024),
         name="mix",
     )(combine, window, total)
     return (mixed, log_total)

time: 65.3 us -> 62.9 us (0.963)
  Pallas kernels: 64.2 us -> 59.5 us
  local copies, waits for them, and re-layouts: 0 us -> 2.53 us
    pallas_call x1, Pallas kernels: 58.3 us -> 55.7 us  [per_device(): pl.pallas_call(functools.partial(dispatch_kernel, nd, nt), out_shape=(jax...]
    unnamed x0 -> x6, local copies, waits for them, and re-layouts: none -> 2.53 us
    pallas_call x1, Pallas kernels: 5.94 us -> 3.77 us  [per_device(): pl.pallas_call(mix_kernel, out_shape=(jax.ShapeDtypeStruct((groups, count...]
where the time goes in v2:
time: 62.9 us; the launch traced here: 62.6 us
  Pallas kernels  59.5 us (95%)
  local copies, waits for them, and re-layouts  2.53 us (4%)
  between operations  0.65 us (1%)
    pallas_call x1, Pallas kernels, per_device(): pl.pallas_call(functools.partial(dispatch_kernel, nd, nt), out_shape=(jax...  55.7 us
    pallas_call x1, Pallas kernels, per_device(): pl.pallas_call(mix_kernel, out_shape=(jax.ShapeDtypeStruct((groups, count...  3.77 us
    unnamed x6, local copies, waits for them, and re-layouts  2.53 us

profile of v2, /device:TPU:0, one launch (start us, length us, event | category | flops | bytes accessed | tf_op | source)
XLA Modules:
  0.0 62.6 jit_solution(11892747911048302370)
XLA Ops:
  0.6 55.7 %dispatch.1 = (bf16[8,96,128]{2,1,0:T(8,128)(2,1)}, bf16[4,6,16,128]{3,2,1,0:T(8,128)(2,1)}, f32[4,8,128]{2,1,0:T(8,128)}) custom-call(bf16[6,512,1024]{2,1,0:T(8,128)(2,1)} %tokens.1, bf16[16,1024]{1,0:T(8,128)(2,1)} %router.1, bf16[1792,4096]{1,0:T(8,128)(2,1)} %bitcast.5, bf16[1792,4096]{1,0:T(8,128)(2,1)} %bitcast.6, bf16[1792,4096]{1,0:T(8,128)(2,1)} %bitcast.7), custom_call_target="tpu_custom_call" | custom-call | tf_op jit(solution)/shard_map/dispatch/pallas_call | solution.py:373
  56.3 0.0 copy-start
  56.3 0.9 %copy-done = bf16[8,96,128]{2,1,0:T(8,128)(2,1)S(1)} copy-done((bf16[8,96,128]{2,1,0:T(8,128)(2,1)S(1)}, bf16[8,96,128]{2,1,0:T(8,128)(2,1)}, u32[]{:S(2)}) %copy-start) | copy-done | bytes 196632
  57.3 0.0 copy-start.1
  57.3 0.9 %copy-done.1 = bf16[4,6,16,128]{3,2,1,0:T(8,128)(2,1)S(1)} copy-done((bf16[4,6,16,128]{3,2,1,0:T(8,128)(2,1)S(1)}, bf16[4,6,16,128]{3,2,1,0:T(8,128)(2,1)}, u32[]{:S(2)}) %copy-start.1) | copy-done | bytes 98328
  58.2 0.0 copy-start.2
  58.2 0.7 %copy-done.2 = f32[4,8,128]{2,1,0:T(8,128)S(1)} copy-done((f32[4,8,128]{2,1,0:T(8,128)S(1)}, f32[4,8,128]{2,1,0:T(8,128)}, u32[]{:S(2)}) %copy-start.2) | copy-done | bytes 16408
  58.9 3.8 %mix.1 = (bf16[6,512,1024]{2,1,0:T(8,128)(2,1)}, f32[6,512]{1,0:T(8,128)}) custom-call(bf16[4,6,16,128]{3,2,1,0:T(8,128)(2,1)S(1)} %copy-done.1, bf16[8,6,16,128]{3,2,1,0:T(8,128)(2,1)S(1)} %bitcast.4, f32[4,8,128]{2,1,0:T(8,128)S(1)} %copy-done.2), custom_call_target="tpu_custom_call" | custom-call | tf_op jit(solution)/shard_map/mix/pallas_call | solution.py:415
Async XLA Ops:
  56.3 0.9 %copy-start = (bf16[8,96,128]{2,1,0:T(8,128)(2,1)S(1)}, bf16[8,96,128]{2,1,0:T(8,128)(2,1)}, u32[]{:S(2)}) copy-start(bf16[8,96,128]{2,1,0:T(8,128)(2,1)} %get-tuple-element.6) | copy-start | bytes 589828
  57.3 0.9 %copy-start.1 = (bf16[4,6,16,128]{3,2,1,0:T(8,128)(2,1)S(1)}, bf16[4,6,16,128]{3,2,1,0:T(8,128)(2,1)}, u32[]{:S(2)}) copy-start(bf16[4,6,16,128]{3,2,1,0:T(8,128)(2,1)} %get-tuple-element.5.combine) | copy-start | bytes 294916
  58.2 0.7 %copy-start.2 = (f32[4,8,128]{2,1,0:T(8,128)S(1)}, f32[4,8,128]{2,1,0:T(8,128)}, u32[]{:S(2)}) copy-start(f32[4,8,128]{2,1,0:T(8,128)} %get-tuple-element.7.total) | copy-start | bytes 49156

commit v3 on v2

--- a/solution.py
+++ b/solution.py
@@ -8,9 +8,10 @@
 from jax.sharding import PartitionSpec as P
 
 SLOTS = 4
-PAD = 32
+ROWS = 16
 LANES = 128
 CHUNKS = 2
+PAD = ROWS * CHUNKS
 WPARTS = 4
 epsilon = 1e-05
 f32 = jnp.float32
@@ -23,9 +24,9 @@
 def dispatch_kernel(
     nd, nt, tokens, router, w_gate, w_up, w_down,
     window_out, combine_out, total_out,
-    tok, wg, wu, wd, stat, stat_in, wbuf, sbuf, stats, pbuf, rbuf, abuf, zin, xin, x_all, hidden,
-    obuf, oin, bbuf, zout,
-    tok_sem, w_sem,
+    tok, wg, wu, wd, stat, stat_in, wbuf, sbuf, stats, pbuf, rbuf, abuf, zin, xin, gate_acc, up_acc, hidden,
+    obuf, oin, bbuf, zout, combine, total_log, mine_out,
+    tok_sem, w_sem, out_sem,
     rs_s, rs_r, ag_s, ag_r, as_s, as_r, cb_s, cb_r, tb_s, tb_r, st_s, st_r, pr_s, pr_r, az_s, az_r, ax_s, ax_r,
     or_s, or_r, bz_s, bz_r, bx_s, bx_r,
 ):
@@ -119,7 +120,7 @@
 
     column = lax.broadcasted_iota(jnp.int32, (16, LANES), 1)
     half = LANES // 2
-    total_out[me_t] = jnp.zeros(total_out.shape[1:], f32)
+    total_log[me_t] = jnp.zeros(total_log.shape[1:], f32)
     for c in range(CHUNKS):
         stat_in[c, me_t] = stat[c, me_t]
         other_tensor(lambda t, c=c: send(
@@ -150,8 +151,8 @@
             row_peak = jnp.max(logits, axis=0, keepdims=True)
             row_powers = jnp.exp(logits - row_peak)
             row_sum = jnp.sum(row_powers, axis=0, keepdims=True)
-            combine_out[me_t, g] = (row_powers / row_sum).astype(bf16)
-            total_out[me_t, g:g + 1, :] = row_peak + jnp.log(row_sum)
+            combine[me_t, g] = (row_powers / row_sum).astype(bf16)
+            total_log[me_t, g:g + 1, :] = row_peak + jnp.log(row_sum)
 
     for c in range(CHUNKS):
         other_tensor(lambda t, c=c: send(
@@ -164,12 +165,8 @@
         for q in range(1, nt):
             csum = csum + factor[q] * pltpu.roll(sbuf[c, q], half, 1)
         mine = jnp.logical_and(column >= c * per, column < (c + 1) * per)
-        if c == 0:
-            stats[me_d, 0] = jnp.where(mine, peak, 0.0)
-            stats[me_d, 1] = jnp.where(mine, csum, 1.0)
-        else:
-            stats[me_d, 0] = jnp.where(mine, peak, stats[me_d, 0])
-            stats[me_d, 1] = jnp.where(mine, csum, stats[me_d, 1])
+        stats[c, me_d, 0] = jnp.where(mine, peak, 0.0)
+        stats[c, me_d, 1] = jnp.where(mine, csum, 1.0)
         other_tensor(lambda t, c=c: send(
             wbuf.at[c, t], wbuf.at[c, t], ag_s.at[c, t], ag_r.at[c, t], "tensor", t).wait_recv())
         for gl in range(per):
@@ -181,62 +178,62 @@
                     preferred_element_type=f32)
             for j in range(owners):
                 pbuf[c, j, gl] = summed[:, j * LANES:(j + 1) * LANES].astype(bf16)
-        if c == CHUNKS - 1:
-            other_owners(lambda j: send(
-                stats.at[me_d], stats.at[me_d], st_s.at[j], st_r.at[me_d], "dp", j).start())
+        other_owners(lambda j, c=c: send(
+            stats.at[c, me_d], stats.at[c, me_d], st_s.at[c, j], st_r.at[c, me_d], "dp", j).start())
         other_owners(lambda j, c=c: send(
             pbuf.at[c, j], rbuf.at[c, me_d], pr_s.at[c, j], pr_r.at[c, me_d], "dp", j).start())
 
     other_tensor(lambda t: send(
-        combine_out.at[me_t], combine_out.at[me_t], cb_s.at[t], cb_r.at[me_t], "tensor", t).start())
-    other_tensor(lambda t: send(
-        total_out.at[me_t], total_out.at[me_t], tb_s.at[t], tb_r.at[me_t], "tensor", t).start())
-
-    def spread_matrix(rows, cols, flip):
-        a = lax.broadcasted_iota(jnp.int32, (rows, cols), 1 if flip else 0)
-        b = lax.broadcasted_iota(jnp.int32, (rows, cols), 0 if flip else 1)
-        k, q = a // PAD, a % PAD
-        source = (q // SLOTS) * 16 + k * SLOTS + q % SLOTS
-        hit = jnp.logical_and(q < groups * SLOTS, source == b)
+        combine.at[me_t], combine.at[me_t], cb_s.at[t], cb_r.at[me_t], "tensor", t).start())
+    other_tensor(lambda t: send(
+        total_log.at[me_t], total_log.at[me_t], tb_s.at[t], tb_r.at[me_t], "tensor", t).start())
+
+    def spread_matrix(chunks, flip):
+        shape = (nt * chunks * ROWS, chunks * per * 16)
+        a = lax.broadcasted_iota(jnp.int32, shape[::-1] if flip else shape, 1 if flip else 0)
+        b = lax.broadcasted_iota(jnp.int32, shape[::-1] if flip else shape, 0 if flip else 1)
+        k, c, q = a // (chunks * ROWS), (a // ROWS) % chunks, a % ROWS
+        source = (c * per + q // SLOTS) * 16 + k * SLOTS + q % SLOTS
+        hit = jnp.logical_and(q < per * SLOTS, source == b)
         return jnp.where(hit, 1.0, 0.0).astype(bf16)
 
-    spread = spread_matrix(nt * PAD, groups * 16, False)
-    gather = spread_matrix(groups * 16, nt * PAD, True)
+    spread = spread_matrix(1, False)
+    gather = spread_matrix(CHUNKS, True)
 
     def reduce_slots():
         for c in range(CHUNKS):
             other_dp(lambda d, c=c: send(
+                stats.at[c, d], stats.at[c, d], st_s.at[c, 0], st_r.at[c, d], "dp", d).wait_recv())
+            peak = stats[c, 0, 0]
+            for i in range(1, nd):
+                peak = jnp.maximum(peak, stats[c, i, 0])
+            factor = [jnp.exp(stats[c, i, 0] - peak) for i in range(nd)]
+            den = factor[0] * stats[c, 0, 1]
+            for i in range(1, nd):
+                den = den + factor[i] * stats[c, i, 1]
+            scale = [f / den for f in factor]
+            other_dp(lambda d, c=c: send(
                 pbuf.at[c, 0], rbuf.at[c, d], pr_s.at[c, 0], pr_r.at[c, d], "dp", d).wait_recv())
             rbuf[c, me_d] = pbuf[c, me_d]
-        other_dp(lambda d: send(
-            stats.at[d], stats.at[d], st_s.at[0], st_r.at[d], "dp", d).wait_recv())
-        peak = stats[0, 0]
-        for i in range(1, nd):
-            peak = jnp.maximum(peak, stats[i, 0])
-        factor = [jnp.exp(stats[i, 0] - peak) for i in range(nd)]
-        den = factor[0] * stats[0, 1]
-        for i in range(1, nd):
-            den = den + factor[i] * stats[i, 1]
-        scale = [f / den for f in factor]
-        rows = []
-        for g in range(groups):
-            c, gl = g // per, g % per
-            acc = jnp.zeros((16, LANES), f32)
-            for i in range(nd):
-                acc = acc + scale[i][:, g:g + 1] * rbuf[c, i, gl].astype(f32)
-            rows.append(acc.astype(bf16))
-        slot_in = jnp.concatenate(rows, axis=0)
-        moved = lax.dot_general(spread, slot_in, NN, preferred_element_type=f32).astype(bf16)
-        for k in range(nt):
-            abuf[k] = moved[k * PAD:(k + 1) * PAD]
-        zin[me_t] = abuf[me_t]
-        other_tensor(lambda t: send(
-            abuf.at[t], zin.at[me_t], az_s.at[t], az_r.at[me_t], "tensor", t).start())
-        other_tensor(lambda t: send(
-            abuf.at[t], zin.at[t], az_s.at[t], az_r.at[t], "tensor", t).wait_recv())
-        xin[me_d] = zin[...]
-        other_dp(lambda d: send(
-            zin, xin.at[me_d], ax_s.at[d], ax_r.at[me_d], "dp", d).start())
+            rows = []
+            for gl in range(per):
+                g = c * per + gl
+                acc = jnp.zeros((16, LANES), f32)
+                for i in range(nd):
+                    acc = acc + scale[i][:, g:g + 1] * rbuf[c, i, gl].astype(f32)
+                rows.append(acc.astype(bf16))
+            slot_in = jnp.concatenate(rows, axis=0)
+            moved = lax.dot_general(spread, slot_in, NN, preferred_element_type=f32).astype(bf16)
+            for k in range(nt):
+                abuf[c, k] = moved[k * ROWS:(k + 1) * ROWS]
+            zin[c, me_t] = abuf[c, me_t]
+            other_tensor(lambda t, c=c: send(
+                abuf.at[c, t], zin.at[c, me_t], az_s.at[c, t], az_r.at[c, me_t], "tensor", t).start())
+            other_tensor(lambda t, c=c: send(
+                abuf.at[c, t], zin.at[c, t], az_s.at[c, t], az_r.at[c, t], "tensor", t).wait_recv())
+            xin[me_d, c] = zin[c]
+            other_dp(lambda d, c=c: send(
+                zin.at[c], xin.at[me_d, c], ax_s.at[c, d], ax_r.at[c, me_d], "dp", d).start())
     if_owner(reduce_slots)
     for c in range(CHUNKS):
         other_tensor(lambda t, c=c: send(
@@ -247,35 +244,49 @@
             sbuf.at[c, me_t], sbuf.at[c, me_t], as_s.at[c, t], as_r.at[c, t], "tensor", t).wait_send())
         other_owners(lambda j, c=c: send(
             pbuf.at[c, j], rbuf.at[c, j], pr_s.at[c, j], pr_r.at[c, j], "dp", j).wait_send())
-    other_owners(lambda j: send(
-        stats.at[me_d], stats.at[me_d], st_s.at[j], st_r.at[j], "dp", j).wait_send())
-    other_tensor(lambda t: send(
-        combine_out.at[me_t], combine_out.at[t], cb_s.at[t], cb_r.at[t], "tensor", t).wait_send())
-    other_tensor(lambda t: send(
-        total_out.at[me_t], total_out.at[t], tb_s.at[t], tb_r.at[t], "tensor", t).wait_send())
-    other_owners(lambda j: send(
-        zin, xin.at[j], ax_s.at[0], ax_r.at[j], "dp", j).wait_recv())
-
-    for i in range(owners):
-        for t in range(nt):
-            x_all[:, t * width + i * LANES:t * width + (i + 1) * LANES] = xin[i, t]
-
+        other_owners(lambda j, c=c: send(
+            stats.at[c, me_d], stats.at[c, me_d], st_s.at[c, j], st_r.at[c, j], "dp", j).wait_send())
+    other_tensor(lambda t: send(
+        combine.at[me_t], combine.at[t], cb_s.at[t], cb_r.at[t], "tensor", t).wait_send())
+    other_tensor(lambda t: send(
+        total_log.at[me_t], total_log.at[t], tb_s.at[t], tb_r.at[t], "tensor", t).wait_send())
     for m in (0, 1):
         for p in range(WPARTS):
             weight_copy(m, p).wait()
+    pairs = owners // 2
     fc = 256 if hidden_here % 256 == 0 else hidden_here
-
-    for f in range(hidden_here // fc):
-        x = x_all[...]
-        gate = lax.dot_general(x, wg[f * fc:(f + 1) * fc, :], NT, preferred_element_type=f32)
-        up = lax.dot_general(x, wu[f * fc:(f + 1) * fc, :], NT, preferred_element_type=f32)
-        act = gate / (1.0 + jnp.exp(-gate)) * up
-        hidden[:, f * fc:(f + 1) * fc] = act.astype(bf16)
+    gate_acc[...] = jnp.zeros(gate_acc.shape, f32)
+    up_acc[...] = jnp.zeros(up_acc.shape, f32)
+
+    def feature_part(k, carry):
+        p = lax.rem(k + me_d // 2, pairs)
+        for h in range(2):
+            j = 2 * p + h
+
+            @pl.when(j != me_d)
+            def _():
+                for c in range(CHUNKS):
+                    send(zin.at[c], xin.at[j, c], ax_s.at[c, 0], ax_r.at[c, j], "dp", j).wait_recv()
+        xs = []
+        for t in range(nt):
+            xs.append(jnp.concatenate([
+                jnp.concatenate([xin[2 * p + h, c, t] for c in range(CHUNKS)], axis=0)
+                for h in range(2)], axis=1))
+        for f in range(hidden_here // fc):
+            rows = slice(f * fc, (f + 1) * fc)
+            for w, acc in ((wg, gate_acc), (wu, up_acc)):
+                part = acc[:, rows]
+                for t in range(nt):
+                    cols = pl.ds(pl.multiple_of(t * width + p * 2 * LANES, 2 * LANES), 2 * LANES)
+                    part = part + lax.dot_general(xs[t], w[rows, cols], NT, preferred_element_type=f32)
+                acc[:, rows] = part
+        return carry
+    lax.fori_loop(0, pairs, feature_part, 0)
+    gate = gate_acc[...]
+    hidden[...] = (gate / (1.0 + jnp.exp(-gate)) * up_acc[...]).astype(bf16)
 
     for p in range(WPARTS):
         weight_copy(2, p).wait()
-
-    pairs = owners // 2
 
     def down_part(k, carry):
         p = lax.rem(k + me_d // 2 + 1, pairs)
@@ -294,15 +305,20 @@
     lax.fori_loop(0, pairs, down_part, 0)
 
     def drain_inputs():
-        other_tensor(lambda t: send(
-            abuf.at[t], zin.at[t], az_s.at[t], az_r.at[t], "tensor", t).wait_send())
-        other_dp(lambda d: send(
-            zin, xin.at[0], ax_s.at[d], ax_r.at[d], "dp", d).wait_send())
+        for c in range(CHUNKS):
+            other_tensor(lambda t, c=c: send(
+                abuf.at[c, t], zin.at[c, t], az_s.at[c, t], az_r.at[c, t], "tensor", t).wait_send())
+            other_dp(lambda d, c=c: send(
+                zin.at[c], xin.at[0, c], ax_s.at[c, d], ax_r.at[c, d], "dp", d).wait_send())
     if_owner(drain_inputs)
     other_tensor(lambda t: send(
-        combine_out.at[t], combine_out.at[t], cb_s.at[t], cb_r.at[t], "tensor", t).wait_recv())
-    other_tensor(lambda t: send(
-        total_out.at[t], total_out.at[t], tb_s.at[t], tb_r.at[t], "tensor", t).wait_recv())
+        combine.at[t], combine.at[t], cb_s.at[t], cb_r.at[t], "tensor", t).wait_recv())
+    other_tensor(lambda t: send(
+        total_log.at[t], total_log.at[t], tb_s.at[t], tb_r.at[t], "tensor", t).wait_recv())
+    combine_write = pltpu.make_async_copy(combine, combine_out, out_sem.at[0])
+    total_write = pltpu.make_async_copy(total_log, total_out, out_sem.at[1])
+    combine_write.start()
+    total_write.start()
 
     def reduce_outputs():
         oin[me_d] = obuf[me_d]
@@ -319,13 +335,14 @@
         other_tensor(lambda t: send(
             bbuf.at[t], zout.at[t], bz_s.at[t], bz_r.at[t], "tensor", t).wait_recv())
         rows = jnp.concatenate([zout[k] for k in range(nt)], axis=0)
-        window_out[me_d] = lax.dot_general(
+        mine_out[...] = lax.dot_general(
             gather, rows, NN, preferred_element_type=f32).astype(bf16)
         other_dp(lambda d: send(
-            window_out.at[me_d], window_out.at[me_d], bx_s.at[d], bx_r.at[me_d], "dp", d).start())
+            mine_out, window_out.at[me_d], bx_s.at[d], bx_r.at[me_d], "dp", d).start())
+        pltpu.make_async_copy(mine_out, window_out.at[me_d], out_sem.at[2]).start()
     if_owner(reduce_outputs)
     other_owners(lambda j: send(
-        window_out.at[j], window_out.at[j], bx_s.at[0], bx_r.at[j], "dp", j).wait_recv())
+        mine_out, window_out.at[j], bx_s.at[0], bx_r.at[j], "dp", j).wait_recv())
 
     other_owners(lambda j: send(
         obuf.at[j], oin.at[j], or_s.at[j], or_r.at[j], "dp", j).wait_send())
@@ -334,17 +351,29 @@
         other_tensor(lambda t: send(
             bbuf.at[t], zout.at[t], bz_s.at[t], bz_r.at[t], "tensor", t).wait_send())
         other_dp(lambda d: send(
-            window_out.at[me_d], window_out.at[me_d], bx_s.at[d], bx_r.at[d], "dp", d).wait_send())
+            mine_out, window_out.at[me_d], bx_s.at[d], bx_r.at[d], "dp", d).wait_send())
+        pltpu.make_async_copy(mine_out, window_out.at[me_d], out_sem.at[2]).wait()
     if_owner(drain)
-
-
-def mix_kernel(combine, window, total, mixed, total_out, held, sem):
+    combine_write.wait()
+    total_write.wait()
+
+
+def mix_kernel(combine_in, window_in, total_in, mixed, total_out, combine, window, total, held, in_sem, sem):
+    loads = [
+        pltpu.make_async_copy(combine_in, combine, in_sem.at[0]),
+        pltpu.make_async_copy(window_in, window, in_sem.at[1]),
+        pltpu.make_async_copy(total_in, total, in_sem.at[2]),
+    ]
+    for load in loads:
+        load.start()
     nt, groups = combine.shape[:2]
     owners, quarter = window.shape[0], combine.shape[3]
 
     def copy(g):
         return pltpu.make_async_copy(held.at[g], mixed.at[g], sem.at[g])
 
+    for load in loads:
+        load.wait()
     for g in range(groups):
         slots = jnp.concatenate([window[j, g] for j in range(owners)], axis=1)
         for q in range(nt):
@@ -370,6 +399,7 @@
     VM, DMA = pltpu.VMEM, pltpu.SemaphoreType.DMA
     any_spec = pl.BlockSpec(memory_space=pl.ANY)
     vmem_spec = pl.BlockSpec(memory_space=pltpu.VMEM)
+    hbm_spec = pl.BlockSpec(memory_space=pltpu.HBM)
     window, combine, total = pl.pallas_call(
         functools.partial(dispatch_kernel, nd, nt),
         out_shape=(
@@ -378,7 +408,7 @@
             jax.ShapeDtypeStruct((nt, 8, quarter), f32),
         ),
         in_specs=[any_spec, vmem_spec, any_spec, any_spec, any_spec],
-        out_specs=(vmem_spec, vmem_spec, vmem_spec),
+        out_specs=(hbm_spec, hbm_spec, hbm_spec),
         scratch_shapes=[
             VM((groups, count, width), bf16),
             VM((hidden_here, full), bf16),
@@ -388,23 +418,27 @@
             VM((CHUNKS, nt, srows, quarter), f32),
             VM((CHUNKS, nt, per, slots, quarter), bf16),
             VM((CHUNKS, nt, slots, LANES), f32),
-            VM((nd, 2, slots, LANES), f32),
+            VM((CHUNKS, nd, 2, slots, LANES), f32),
             VM((CHUNKS, owners, per, slots, LANES), bf16),
             VM((CHUNKS, nd, per, slots, LANES), bf16),
-            VM((nt, PAD, LANES), bf16),
-            VM((nt, PAD, LANES), bf16),
-            VM((owners, nt, PAD, LANES), bf16),
-            VM((PAD, full), bf16),
+            VM((CHUNKS, nt, ROWS, LANES), bf16),
+            VM((CHUNKS, nt, ROWS, LANES), bf16),
+            VM((owners, CHUNKS, nt, ROWS, LANES), bf16),
+            VM((PAD, hidden_here), f32),
+            VM((PAD, hidden_here), f32),
             VM((PAD, hidden_here), bf16),
             VM((owners, nt, PAD, LANES), bf16),
             VM((nd, nt, PAD, LANES), bf16),
             VM((nt, PAD, LANES), bf16),
             VM((nt, PAD, LANES), bf16),
-            DMA((groups,)), DMA((3, WPARTS)),
+            VM((nt, groups, slots, quarter), bf16),
+            VM((nt, 8, quarter), f32),
+            VM((groups * slots, LANES), bf16),
+            DMA((groups,)), DMA((3, WPARTS)), DMA((3,)),
             DMA((CHUNKS, nt)), DMA((CHUNKS, nt)), DMA((CHUNKS, nt)), DMA((CHUNKS, nt)),
             DMA((CHUNKS, nt)), DMA((CHUNKS, nt)), DMA((nt,)), DMA((nt,)), DMA((nt,)), DMA((nt,)),
-            DMA((owners,)), DMA((nd,)), DMA((CHUNKS, owners)), DMA((CHUNKS, nd)),
-            DMA((nt,)), DMA((nt,)), DMA((nd,)), DMA((owners,)),
+            DMA((CHUNKS, owners)), DMA((CHUNKS, nd)), DMA((CHUNKS, owners)), DMA((CHUNKS, nd)),
+            DMA((CHUNKS, nt)), DMA((CHUNKS, nt)), DMA((CHUNKS, nd)), DMA((CHUNKS, owners)),
             DMA((owners,)), DMA((nd,)), DMA((nt,)), DMA((nt,)), DMA((nd,)), DMA((owners,)),
         ],
         compiler_params=pltpu.CompilerParams(
@@ -418,10 +452,13 @@
             jax.ShapeDtypeStruct((groups, count, width), bf16),
             jax.ShapeDtypeStruct((groups, count), f32),
         ),
-        in_specs=[vmem_spec, vmem_spec, vmem_spec],
+        in_specs=[hbm_spec, hbm_spec, hbm_spec],
         out_specs=(any_spec, vmem_spec),
-        scratch_shapes=[VM((groups, count, width), bf16), DMA((groups,))],
-        compiler_params=pltpu.CompilerParams(vmem_limit_bytes=32 * 1024 * 1024),
+        scratch_shapes=[
+            VM(combine.shape, bf16), VM(window.shape, bf16), VM(total.shape, f32),
+            VM((groups, count, width), bf16), DMA((3,)), DMA((groups,)),
+        ],
+        compiler_params=pltpu.CompilerParams(vmem_limit_bytes=60 * 1024 * 1024),
         name="mix",
     )(combine, window, total)
     return (mixed, log_total)

time: 62.9 us -> 60.9 us (0.968)
  local copies, waits for them, and re-layouts: 2.53 us -> 0 us
    unnamed x6 -> x0, local copies, waits for them, and re-layouts: 2.53 us -> none
    pallas_call x1, Pallas kernels: 3.77 us -> 4.78 us  [per_device(): pl.pallas_call(mix_kernel, out_shape=(jax.ShapeDtypeStruct((groups, count...]
where the time goes in v3:
time: 60.9 us; the launch traced here: 60.7 us
  Pallas kernels  60.1 us (99%)
  between operations  0.64 us (1%)
    pallas_call x1, Pallas kernels, per_device(): pl.pallas_call(functools.partial(dispatch_kernel, nd, nt), out_shape=(jax...  55.3 us
    pallas_call x1, Pallas kernels, per_device(): pl.pallas_call(mix_kernel, out_shape=(jax.ShapeDtypeStruct((groups, count...  4.78 us

profile of v3, /device:TPU:0, one launch (start us, length us, event | category | flops | bytes accessed | tf_op | source)
XLA Modules:
  0.0 60.7 jit_solution(672482425912481161)
XLA Ops:
  0.6 55.3 %dispatch.1 = (bf16[8,96,128]{2,1,0:T(8,128)(2,1)}, bf16[4,6,16,128]{3,2,1,0:T(8,128)(2,1)}, f32[4,8,128]{2,1,0:T(8,128)}) custom-call(bf16[6,512,1024]{2,1,0:T(8,128)(2,1)} %tokens.1, bf16[16,1024]{1,0:T(8,128)(2,1)} %router.1, bf16[1792,4096]{1,0:T(8,128)(2,1)} %bitcast.4, bf16[1792,4096]{1,0:T(8,128)(2,1)} %bitcast.5, bf16[1792,4096]{1,0:T(8,128)(2,1)} %bitcast.6), custom_call_target="tpu_custom_call" | custom-call | tf_op jit(solution)/shard_map/dispatch/pallas_call | solution.py:403
  56.0 4.8 %mix.1 = (bf16[6,512,1024]{2,1,0:T(8,128)(2,1)}, f32[6,512]{1,0:T(8,128)}) custom-call(bf16[4,6,16,128]{3,2,1,0:T(8,128)(2,1)} %get-tuple-element.5.combine_in, bf16[8,6,16,128]{3,2,1,0:T(8,128)(2,1)} %bitcast.7, f32[4,8,128]{2,1,0:T(8,128)} %get-tuple-element.7.total_in), custom_call_target="tpu_custom_call" | custom-call | tf_op jit(solution)/shard_map/mix/pallas_call | solution.py:449

commit v4 on v3

--- a/solution.py
+++ b/solution.py
@@ -82,6 +82,9 @@
 
     for g in range(groups):
         token_copy(g).start()
+    for m in range(3):
+        for p in range(WPARTS):
+            weight_copy(m, p).start()
 
     barrier = pltpu.get_barrier_semaphore()
     other_tensor(lambda t: pl.semaphore_signal(
@@ -111,12 +114,6 @@
             pl.semaphore_wait(barrier, nt - 1 + nd - 1)
         other_tensor(lambda t, c=c: send(
             stat.at[c, t], stat_in.at[c, me_t], rs_s.at[c, t], rs_r.at[c, me_t], "tensor", t).start())
-        if c == 0:
-            for p in range(WPARTS):
-                weight_copy(0, p).start()
-    for m in (1, 2):
-        for p in range(WPARTS):
-            weight_copy(m, p).start()
 
     column = lax.broadcasted_iota(jnp.int32, (16, LANES), 1)
     half = LANES // 2
@@ -140,7 +137,7 @@
             csum = jnp.sum(powers, axis=1, keepdims=True)
             wbuf[c, me_t, gl] = (powers * norm[gl:gl + 1]).astype(bf16)
             summary = jnp.where(column == g, peak, jnp.where(column == half + g, csum, summary))
-        sbuf[c, me_t] = summary
+        sbuf[c, me_t] = summary[:8] + pltpu.roll(summary[8:], LANES // 4, 1)
         other_tensor(lambda t, c=c: send(
             sbuf.at[c, me_t], sbuf.at[c, me_t], as_s.at[c, t], as_r.at[c, me_t], "tensor", t).start())
         other_tensor(lambda t, c=c: send(
@@ -154,6 +151,14 @@
             combine[me_t, g] = (row_powers / row_sum).astype(bf16)
             total_log[me_t, g:g + 1, :] = row_peak + jnp.log(row_sum)
 
+    fold = LANES // 4
+    lane = lax.broadcasted_iota(jnp.int32, (8, LANES), 1)
+
+    def slot_column(tile, g):
+        low = jnp.sum(jnp.where(lane == g, tile, 0.0), axis=1, keepdims=True)
+        high = jnp.sum(jnp.where(lane == fold + g, tile, 0.0), axis=1, keepdims=True)
+        return jnp.concatenate([low, high], axis=0)
+
     for c in range(CHUNKS):
         other_tensor(lambda t, c=c: send(
             sbuf.at[c, t], sbuf.at[c, t], as_s.at[c, t], as_r.at[c, t], "tensor", t).wait_recv())
@@ -164,29 +169,27 @@
         csum = factor[0] * pltpu.roll(sbuf[c, 0], half, 1)
         for q in range(1, nt):
             csum = csum + factor[q] * pltpu.roll(sbuf[c, q], half, 1)
-        mine = jnp.logical_and(column >= c * per, column < (c + 1) * per)
-        stats[c, me_d, 0] = jnp.where(mine, peak, 0.0)
-        stats[c, me_d, 1] = jnp.where(mine, csum, 1.0)
+        place = lane % fold
+        mine = jnp.logical_and(lane < half, jnp.logical_and(place >= c * per, place < (c + 1) * per))
+        stats[c, me_d] = jnp.where(mine, peak, 0.0) + pltpu.roll(jnp.where(mine, csum, 0.0), half, 1)
+        other_owners(lambda j, c=c: send(
+            stats.at[c, me_d], stats.at[c, me_d], st_s.at[c, j], st_r.at[c, me_d], "dp", j).start())
         other_tensor(lambda t, c=c: send(
             wbuf.at[c, t], wbuf.at[c, t], ag_s.at[c, t], ag_r.at[c, t], "tensor", t).wait_recv())
-        for gl in range(per):
+
+        def weigh(gl, carry, c=c, factor=factor):
             g = c * per + gl
             summed = jnp.zeros((16, width), f32)
             for q in range(nt):
-                summed = summed + factor[q][:, g:g + 1] * lax.dot_general(
+                summed = summed + slot_column(factor[q], g) * lax.dot_general(
                     wbuf[c, q, gl], tok[g, q * quarter:(q + 1) * quarter, :], NN,
                     preferred_element_type=f32)
             for j in range(owners):
                 pbuf[c, j, gl] = summed[:, j * LANES:(j + 1) * LANES].astype(bf16)
-        other_owners(lambda j, c=c: send(
-            stats.at[c, me_d], stats.at[c, me_d], st_s.at[c, j], st_r.at[c, me_d], "dp", j).start())
+            return carry
+        lax.fori_loop(0, per, weigh, 0)
         other_owners(lambda j, c=c: send(
             pbuf.at[c, j], rbuf.at[c, me_d], pr_s.at[c, j], pr_r.at[c, me_d], "dp", j).start())
-
-    other_tensor(lambda t: send(
-        combine.at[me_t], combine.at[me_t], cb_s.at[t], cb_r.at[me_t], "tensor", t).start())
-    other_tensor(lambda t: send(
-        total_log.at[me_t], total_log.at[me_t], tb_s.at[t], tb_r.at[me_t], "tensor", t).start())
 
     def spread_matrix(chunks, flip):
         shape = (nt * chunks * ROWS, chunks * per * 16)
@@ -204,13 +207,13 @@
         for c in range(CHUNKS):
             other_dp(lambda d, c=c: send(
                 stats.at[c, d], stats.at[c, d], st_s.at[c, 0], st_r.at[c, d], "dp", d).wait_recv())
-            peak = stats[c, 0, 0]
+            peak = stats[c, 0]
             for i in range(1, nd):
-                peak = jnp.maximum(peak, stats[c, i, 0])
-            factor = [jnp.exp(stats[c, i, 0] - peak) for i in range(nd)]
-            den = factor[0] * stats[c, 0, 1]
+                peak = jnp.maximum(peak, stats[c, i])
+            factor = [jnp.exp(stats[c, i] - peak) for i in range(nd)]
+            den = factor[0] * pltpu.roll(stats[c, 0], half, 1)
             for i in range(1, nd):
-                den = den + factor[i] * stats[c, i, 1]
+                den = den + factor[i] * pltpu.roll(stats[c, i], half, 1)
             scale = [f / den for f in factor]
             other_dp(lambda d, c=c: send(
                 pbuf.at[c, 0], rbuf.at[c, d], pr_s.at[c, 0], pr_r.at[c, d], "dp", d).wait_recv())
@@ -220,7 +223,9 @@
                 g = c * per + gl
                 acc = jnp.zeros((16, LANES), f32)
                 for i in range(nd):
-                    acc = acc + scale[i][:, g:g + 1] * rbuf[c, i, gl].astype(f32)
+                    column_scale = jnp.concatenate(
+                        [scale[i][:, g:g + 1], scale[i][:, fold + g:fold + g + 1]], axis=0)
+                    acc = acc + column_scale * rbuf[c, i, gl].astype(f32)
                 rows.append(acc.astype(bf16))
             slot_in = jnp.concatenate(rows, axis=0)
             moved = lax.dot_general(spread, slot_in, NN, preferred_element_type=f32).astype(bf16)
@@ -235,6 +240,12 @@
             other_dp(lambda d, c=c: send(
                 zin.at[c], xin.at[me_d, c], ax_s.at[c, d], ax_r.at[c, me_d], "dp", d).start())
     if_owner(reduce_slots)
+
+    other_tensor(lambda t: send(
+        combine.at[me_t], combine.at[me_t], cb_s.at[t], cb_r.at[me_t], "tensor", t).start())
+    other_tensor(lambda t: send(
+        total_log.at[me_t], total_log.at[me_t], tb_s.at[t], tb_r.at[me_t], "tensor", t).start())
+
     for c in range(CHUNKS):
         other_tensor(lambda t, c=c: send(
             stat.at[c, t], stat_in.at[c, t], rs_s.at[c, t], rs_r.at[c, t], "tensor", t).wait_send())
@@ -374,13 +385,15 @@
 
     for load in loads:
         load.wait()
-    for g in range(groups):
+
+    def mix_group(g, carry):
         slots = jnp.concatenate([window[j, g] for j in range(owners)], axis=1)
-        for q in range(nt):
-            held[g, q * quarter:(q + 1) * quarter, :] = lax.dot_general(
-                combine[q, g], slots, (((0,), (0,)), ((), ())),
-                preferred_element_type=f32).astype(bf16)
+        rows = jnp.concatenate([combine[q, g] for q in range(nt)], axis=1)
+        held[g] = lax.dot_general(
+            rows, slots, (((0,), (0,)), ((), ())), preferred_element_type=f32).astype(bf16)
         copy(g).start()
+        return carry
+    lax.fori_loop(0, groups, mix_group, 0)
     for q in range(nt):
         total_out[:, q * quarter:(q + 1) * quarter] = total[q, :groups, :]
     for g in range(groups):
@@ -417,8 +430,8 @@
             VM((CHUNKS, nt, srows, quarter), f32),
             VM((CHUNKS, nt, srows, quarter), f32),
             VM((CHUNKS, nt, per, slots, quarter), bf16),
-            VM((CHUNKS, nt, slots, LANES), f32),
-            VM((CHUNKS, nd, 2, slots, LANES), f32),
+            VM((CHUNKS, nt, 8, LANES), f32),
+            VM((CHUNKS, nd, 8, LANES), f32),
             VM((CHUNKS, owners, per, slots, LANES), bf16),
             VM((CHUNKS, nd, per, slots, LANES), bf16),
             VM((CHUNKS, nt, ROWS, LANES), bf16),

time: 60.9 us -> 69.4 us (1.14)
  Pallas kernels: 60.1 us -> 68.5 us
    pallas_call x1, Pallas kernels: 55.3 us -> 63.2 us  [per_device(): pl.pallas_call(functools.partial(dispatch_kernel, nd, nt), out_shape=(jax...]
where the time goes in v4:
time: 69.4 us; the launch traced here: 69.2 us
  Pallas kernels  68.5 us (99%)
    pallas_call x1, Pallas kernels, per_device(): pl.pallas_call(functools.partial(dispatch_kernel, nd, nt), out_shape=(jax...  63.2 us
    pallas_call x1, Pallas kernels, per_device(): pl.pallas_call(mix_kernel, out_shape=(jax.ShapeDtypeStruct((groups, count...  5.36 us

profile of v4, /device:TPU:0, one launch (start us, length us, event | category | flops | bytes accessed | tf_op | source)
XLA Modules:
  0.0 69.2 jit_solution(14091784502946475504)
XLA Ops:
  0.6 63.2 %dispatch.1 = (bf16[8,96,128]{2,1,0:T(8,128)(2,1)}, bf16[4,6,16,128]{3,2,1,0:T(8,128)(2,1)}, f32[4,8,128]{2,1,0:T(8,128)}) custom-call(bf16[6,512,1024]{2,1,0:T(8,128)(2,1)} %tokens.1, bf16[16,1024]{1,0:T(8,128)(2,1)} %router.1, bf16[1792,4096]{1,0:T(8,128)(2,1)} %bitcast.4, bf16[1792,4096]{1,0:T(8,128)(2,1)} %bitcast.5, bf16[1792,4096]{1,0:T(8,128)(2,1)} %bitcast.6), custom_call_target="tpu_custom_call" | custom-call | tf_op jit(solution)/shard_map/dispatch/pallas_call | solution.py:416
  63.8 5.4 %mix.1 = (bf16[6,512,1024]{2,1,0:T(8,128)(2,1)}, f32[6,512]{1,0:T(8,128)}) custom-call(bf16[4,6,16,128]{3,2,1,0:T(8,128)(2,1)} %get-tuple-element.5.combine_in, bf16[8,6,16,128]{3,2,1,0:T(8,128)(2,1)} %bitcast.7, f32[4,8,128]{2,1,0:T(8,128)} %get-tuple-element.7.total_in), custom_call_target="tpu_custom_call" | custom-call | tf_op jit(solution)/shard_map/mix/pallas_call | solution.py:462

commit v5 on v4

--- a/solution.py
+++ b/solution.py
@@ -12,7 +12,7 @@
 LANES = 128
 CHUNKS = 2
 PAD = ROWS * CHUNKS
-WPARTS = 4
+WPARTS = 7
 epsilon = 1e-05
 f32 = jnp.float32
 bf16 = jnp.bfloat16
@@ -82,9 +82,12 @@
 
     for g in range(groups):
         token_copy(g).start()
-    for m in range(3):
-        for p in range(WPARTS):
-            weight_copy(m, p).start()
+    pieces = [(m, p) for m in range(3) for p in range(WPARTS)]
+
+    def start_weights(n):
+        for m, p in pieces[:n]:
+            weight_copy(m, p).start(priority=1)
+        del pieces[:n]
 
     barrier = pltpu.get_barrier_semaphore()
     other_tensor(lambda t: pl.semaphore_signal(
@@ -114,6 +117,7 @@
             pl.semaphore_wait(barrier, nt - 1 + nd - 1)
         other_tensor(lambda t, c=c: send(
             stat.at[c, t], stat_in.at[c, me_t], rs_s.at[c, t], rs_r.at[c, me_t], "tensor", t).start())
+        start_weights(3)
 
     column = lax.broadcasted_iota(jnp.int32, (16, LANES), 1)
     half = LANES // 2
@@ -142,6 +146,7 @@
             sbuf.at[c, me_t], sbuf.at[c, me_t], as_s.at[c, t], as_r.at[c, me_t], "tensor", t).start())
         other_tensor(lambda t, c=c: send(
             wbuf.at[c, me_t], wbuf.at[c, me_t], ag_s.at[c, t], ag_r.at[c, me_t], "tensor", t).start())
+        start_weights(3 if c == 0 else 4)
         for gl in range(per):
             g = c * per + gl
             logits = all_logits[gl]
@@ -190,6 +195,7 @@
         lax.fori_loop(0, per, weigh, 0)
         other_owners(lambda j, c=c: send(
             pbuf.at[c, j], rbuf.at[c, me_d], pr_s.at[c, j], pr_r.at[c, me_d], "dp", j).start())
+        start_weights(2 if c == 0 else 3)
 
     def spread_matrix(chunks, flip):
         shape = (nt * chunks * ROWS, chunks * per * 16)
@@ -240,6 +246,7 @@
             other_dp(lambda d, c=c: send(
                 zin.at[c], xin.at[me_d, c], ax_s.at[c, d], ax_r.at[c, me_d], "dp", d).start())
     if_owner(reduce_slots)
+    start_weights(len(pieces))
 
     other_tensor(lambda t: send(
         combine.at[me_t], combine.at[me_t], cb_s.at[t], cb_r.at[me_t], "tensor", t).start())

time: 69.4 us -> 61.1 us (0.88)
  Pallas kernels: 68.5 us -> 60.3 us
    pallas_call x1, Pallas kernels: 63.2 us -> 54.9 us  [per_device(): pl.pallas_call(functools.partial(dispatch_kernel, nd, nt), out_shape=(jax...]
where the time goes in v5:
time: 61.1 us; the launch traced here: 60.9 us
  Pallas kernels  60.3 us (99%)
  between operations  0.64 us (1%)
    pallas_call x1, Pallas kernels, per_device(): pl.pallas_call(functools.partial(dispatch_kernel, nd, nt), out_shape=(jax...  54.9 us
    pallas_call x1, Pallas kernels, per_device(): pl.pallas_call(mix_kernel, out_shape=(jax.ShapeDtypeStruct((groups, count...  5.36 us

profile of v5, /device:TPU:0, one launch (start us, length us, event | category | flops | bytes accessed | tf_op | source)
XLA Modules:
  0.0 60.9 jit_solution(7811779875485461615)
XLA Ops:
  0.6 54.9 %dispatch.1 = (bf16[8,96,128]{2,1,0:T(8,128)(2,1)}, bf16[4,6,16,128]{3,2,1,0:T(8,128)(2,1)}, f32[4,8,128]{2,1,0:T(8,128)}) custom-call(bf16[6,512,1024]{2,1,0:T(8,128)(2,1)} %tokens.1, bf16[16,1024]{1,0:T(8,128)(2,1)} %router.1, bf16[1792,4096]{1,0:T(8,128)(2,1)} %bitcast.4, bf16[1792,4096]{1,0:T(8,128)(2,1)} %bitcast.5, bf16[1792,4096]{1,0:T(8,128)(2,1)} %bitcast.6), custom_call_target="tpu_custom_call" | custom-call | tf_op jit(solution)/shard_map/dispatch/pallas_call | solution.py:423
  55.6 5.4 %mix.1 = (bf16[6,512,1024]{2,1,0:T(8,128)(2,1)}, f32[6,512]{1,0:T(8,128)}) custom-call(bf16[4,6,16,128]{3,2,1,0:T(8,128)(2,1)} %get-tuple-element.5.combine_in, bf16[8,6,16,128]{3,2,1,0:T(8,128)(2,1)} %bitcast.7, f32[4,8,128]{2,1,0:T(8,128)} %get-tuple-element.7.total_in), custom_call_target="tpu_custom_call" | custom-call | tf_op jit(solution)/shard_map/mix/pallas_call | solution.py:469
